TPU v7x, 32 devices: a whole 2x2x4 slice. The times are simulated.
32 devices in a mesh: beam: 2 (over y), sub: 8 (over z, x), tm: 2 (over core).
Axes of the slice: x: 2, y: 2, z: 4, core: 2. Of those that a mesh axis runs over, the one named last changes fastest.
Arguments:
- filterbank: bfloat16 [2048, 1024], P(('beam', 'sub'), 'tm'), parts along dimension 0, may hold values from -6 to 6
- bandpass: float32 [2048], P(('beam', 'sub')), parts along dimension 0, may hold values from 0.3 to 3
- local_delays: int32 [7, 1024], P(None, 'sub'), may hold values from 0 to 32, as said below
- cross_delays: int32 [3, 128], P(None, 'sub'), may hold values from 0 to 32, as said below
Outputs:
- dedispersed: float32 [256, 1024], P(('beam', 'sub'), 'tm'), parts along dimension 0
There are 2 independent parts, one for each index of `beam`. A program takes and returns all parts, laid end to end along the dimension named above; an argument that names none is the same for every part. Nothing has to cross between parts.
Inputs may be any that keep to these rules, and one draw needn't show every extreme that they name: `local_delays`: whole samples; level m of the local levels reads its first entries of each block of 128. `cross_delays`: whole samples.
All inputs are finite; a program needn't handle non-finite values.
Results may differ from a plain program's by a relative error of at most 0.0003.
Values may be sent and summed in bfloat16 or wider, within the bound.
No kernel may reach another device: no remote copies, remote signals or barrier semaphores. Data moves between devices by JAX's collectives and lax.ppermute only.
A program may use at most 64 MiB of HBM per device.

v0:
```python
import functools
import math

import jax
import jax.numpy as jnp
from jax import lax
from jax.experimental import pallas as pl
from jax.experimental.pallas import tpu as pltpu
from jax.sharding import PartitionSpec as P

LANES = 128
SUBLANES = 8
WINDOW = 31
HALF = WINDOW // 2


def iota(shape, axis):
    return lax.broadcasted_iota(jnp.int32, shape, axis)


def turned(x, index, axis):
    return jnp.take_along_axis(x, index, axis=axis, mode="promise_in_bounds")


def blocks_of(columns):
    return -(-columns // LANES)


def later(tiles, shift, count):
    source = iota(shift.shape, 1) - shift
    index = source & (LANES - 1)
    zero = jnp.zeros(shift.shape, jnp.float32)
    spun = [zero] + [turned(tile, index, 1) for tile in tiles]
    return [jnp.where(source >= 0, spun[b + 1], spun[b]) for b in range(count)]


def folded(tiles):
    row = iota(tiles[0].shape, 0)
    reach = SUBLANES // 2
    while reach:
        first = row & reach == 0
        tiles = [
            jnp.where(
                first,
                a + pltpu.roll(a, SUBLANES - reach, 0),
                b + pltpu.roll(b, reach, 0),
            )
            for a, b in zip(tiles[:reach], tiles[reach:])
        ]
        reach //= 2
    return tiles[0]


def table_kernel(*refs):
    fb_ref, *sources = refs[:4]
    own_ref, shifts_ref, gain_ref, steps_ref, band_ref = refs[4:9]
    held, sems = refs[9:12], refs[12]
    copies = [
        pltpu.make_async_copy(a, b, sems.at[i])
        for i, (a, b) in enumerate(zip([*sources, fb_ref], [*held, own_ref]))
    ]
    for copy in copies:
        copy.start()
    bp_ref, ld_ref, cd_ref = held
    rows = own_ref.shape[0]
    local_levels = ld_ref.shape[0]
    cross_levels, trials = cd_ref.shape
    grow = trials.bit_length() - 1
    parity = row_half(cross_levels)
    square = (rows, LANES)
    lane, row = iota(square, 1), iota(square, 0)
    inner, outer = row & (SUBLANES - 1), row >> 3
    half = (rows // 2, LANES)
    lane_h, row_h = iota(half, 1), iota(half, 0)
    inner_h, outer_h = row_h & (SUBLANES - 1), (row_h >> 3) * 2 + parity

    at, to = iota(band_ref.shape, 0) - LANES, iota(band_ref.shape, 1)
    band = jnp.where(at == to, float(WINDOW), 0.0) - jnp.where(jnp.abs(at - to) <= HALF, 1.0, 0.0)
    band_ref[...] = band.astype(jnp.bfloat16)
    pick = lane == inner * trials + outer
    pick_h = lane_h == inner_h * trials + outer_h
    uses = []
    for bit in range(local_levels - grow):
        uses.append((lane_h == (inner_h >> (bit + 1)) * trials + outer_h) & (inner_h >> bit & 1 == 1))
    on, off = jnp.ones((LANES, LANES), jnp.bfloat16), jnp.zeros((LANES, LANES), jnp.bfloat16)
    ones = jnp.concatenate(
        [jnp.concatenate([on, off], axis=1), jnp.concatenate([off, on], axis=1)], axis=0
    )

    for copy in copies[:-1]:
        copy.wait()
    tail = jnp.zeros(half, jnp.int32)
    for bit, use in enumerate(uses):
        tail = tail + jnp.where(use, ld_ref[grow + bit : grow + bit + 1, :], 0)
    parts = [jnp.where(pick_h, ld_ref[m : m + 1, :], 0) for m in range(grow)]
    parts += [tail] + [jnp.zeros(half, jnp.int32)] * ((grow + 1) % 2)
    parts = [part.astype(jnp.float32).astype(jnp.bfloat16) for part in parts]
    pieces = [jnp.concatenate(parts[i : i + 2], axis=0) for i in range(0, len(parts), 2)]
    rest = bp_ref[...]
    for _ in range(3):
        part = rest.astype(jnp.bfloat16).astype(jnp.float32)
        rest = rest - part
        pieces.append(jnp.where(pick, part, 0.0).astype(jnp.bfloat16))
    pieces += [off] * (len(pieces) % 2)
    pairs = [jnp.concatenate(pieces[i : i + 2], axis=1) for i in range(0, len(pieces), 2)]
    spread = jnp.dot(jnp.concatenate(pairs, axis=0), ones, preferred_element_type=jnp.float32)
    spread = [
        spread[i // 2 * rows : (i // 2 + 1) * rows, i % 2 * LANES : (i % 2 + 1) * LANES]
        for i in range(len(pieces))
    ]
    count = len(parts) // 2
    for i in range(count):
        shifts_ref[i * rows : (i + 1) * rows, :] = spread[i].astype(jnp.int32)
    gain_ref[...] = (spread[count] + spread[count + 1] + spread[count + 2]) * (1.0 / WINDOW)
    kept = (SUBLANES, trials)
    kept = iota(kept, 1) == iota(kept, 0) * 2 + parity
    for l in range(cross_levels):
        step = jnp.sum(jnp.where(kept, cd_ref[l : l + 1, :].astype(jnp.float32), 0.0), axis=1, keepdims=True)
        step = jnp.broadcast_to(step, (SUBLANES, LANES)).astype(jnp.int32)
        steps_ref[l * SUBLANES : (l + 1) * SUBLANES, :] = step
    copies[-1].wait()


def plane_kernel(trials, own_ref, other_ref, shifts_ref, gain_ref, band_ref, out_ref, whole_ref, level_ref):
    rows, span = own_ref.shape
    grow = trials.bit_length() - 1
    columns = whole_ref.shape[1]
    blocks = columns // LANES
    first_span = lax.axis_index("tm") == 0

    @pl.when(first_span)
    def _():
        whole_ref[:, :span] = own_ref[...]
        whole_ref[:, span:] = other_ref[...]

    @pl.when(jnp.logical_not(first_span))
    def _():
        whole_ref[:, :span] = other_ref[...]
        whole_ref[:, span:] = own_ref[...]

    for block in range(0, blocks, 2):
        low, high = max(block - 1, 0), min(block + 3, blocks)
        part = band_ref[(low - block + 1) * LANES : (high - block + 1) * LANES, :]
        got = jnp.dot(
            whole_ref[:, low * LANES : high * LANES], part, preferred_element_type=jnp.float32
        )
        level_ref[block * rows : (block + 1) * rows, :] = got[:, :LANES]
        level_ref[(block + 1) * rows : (block + 2) * rows, :] = got[:, LANES:]

    bands = []
    for e in range(trials):
        scale = gain_ref[e * SUBLANES : (e + 1) * SUBLANES, :]
        bands.append(
            [level_ref[pl.ds(block * rows + e, SUBLANES, stride=trials), :] * scale for block in range(blocks)]
        )
    plane = [bands]

    def merged(low, high, at_row):
        moved = later(high, shifts_ref[at_row : at_row + SUBLANES, :], blocks)
        return [a + b for a, b in zip(low, moved)]

    for m in range(grow):
        old, plane = plane, []
        for c in range(2 if m else 1):
            for i, held in enumerate(old):
                j = c * len(old) + i
                starts = [m * rows // 2 + ((e << m) + j) * SUBLANES for e in range(len(held) // 2)]
                plane.append([merged(held[2 * e], held[2 * e + 1], start) for e, start in enumerate(starts)])
    for j, held in enumerate(plane):
        at_row = grow * rows // 2 + j * SUBLANES
        moved = later(held[0], shifts_ref[at_row : at_row + SUBLANES, :], blocks)
        out_ref[pl.ds(j, SUBLANES, stride=SUBLANES), :] = folded(moved)


def row_half(cross_levels):
    half = lax.axis_index("tm")
    for level in range(cross_levels):
        half = half ^ (lax.axis_index("sub") >> level & 1)
    return half


def tile_of(ref, block):
    return ref[block * SUBLANES : (block + 1) * SUBLANES, :]


def merge_kernel(level, scale, own_ref, there_ref, steps_ref, out_ref, send_ref=None):
    is_upper = lax.axis_index("sub") >> level & 1 == 1
    blocks = own_ref.shape[0] // SUBLANES
    lower, upper = [], []
    for block in range(blocks):
        own, there = tile_of(own_ref, block), tile_of(there_ref, block)
        lower.append(jnp.where(is_upper, there, own))
        upper.append(jnp.where(is_upper, own, there))
    moved = later(upper, tile_of(steps_ref, level), blocks)
    new = [a + b for a, b in zip(lower, moved)]
    if scale is None:
        for block in range(blocks):
            out_ref[block * SUBLANES : (block + 1) * SUBLANES, :] = new[block]
        return
    first_span = lax.axis_index("tm") == 0
    past = blocks // 2
    for block in range(past):
        early, late = new[block] * scale, new[block + past] * scale
        out_ref[block * SUBLANES : (block + 1) * SUBLANES, :] = jnp.where(first_span, early, late)
        send_ref[block * SUBLANES : (block + 1) * SUBLANES, :] = jnp.where(first_span, late, early)


def last_kernel(cross_levels, keep_ref, there_ref, out_ref):
    is_even = row_half(cross_levels) == 0
    row = iota((SUBLANES, LANES), 0)
    for block in range(keep_ref.shape[0] // SUBLANES):
        keep, there = tile_of(keep_ref, block), tile_of(there_ref, block)
        even, odd = jnp.where(is_even, keep, there), jnp.where(is_even, there, keep)
        for part in range(2):
            source = (row >> 1) + part * (SUBLANES // 2)
            new = jnp.where(row & 1 == 0, turned(even, source, 0), turned(odd, source, 0))
            out_ref[part * SUBLANES : (part + 1) * SUBLANES, block * LANES : (block + 1) * LANES] = new


def shards(filterbank, bandpass, local_delays, cross_delays):
    rows, span = filterbank.shape
    cross_levels, trials = cross_delays.shape
    subs, spans = lax.axis_size("sub"), lax.axis_size("tm")
    local_levels = local_delays.shape[0]
    shift_max = span // 16
    grow = trials.bit_length() - 1
    past = span // LANES
    assert rows == LANES == trials * SUBLANES and trials == 2 * SUBLANES
    assert spans * past == SUBLANES and (local_levels - grow) * shift_max < LANES

    vmem = pl.BlockSpec(memory_space=pltpu.VMEM)
    tiled = lambda count, kind=jnp.float32: jax.ShapeDtypeStruct((count * SUBLANES, LANES), kind)
    room = lambda size: pltpu.CompilerParams(vmem_limit_bytes=size << 20)
    call = functools.partial(pl.pallas_call, compiler_params=room(1))
    swap = [(0, 1), (1, 0)]
    other = lax.ppermute(filterbank, "tm", swap)
    args = (filterbank, bandpass[None, :], local_delays, cross_delays)
    own, shifts, gain, steps, band = pl.pallas_call(
        table_kernel,
        out_shape=(
            jax.ShapeDtypeStruct(filterbank.shape, filterbank.dtype),
            tiled((grow + 2) // 2 * trials, jnp.int32),
            tiled(trials),
            tiled(cross_levels, jnp.int32),
            jax.ShapeDtypeStruct((4 * LANES, 2 * LANES), jnp.bfloat16),
        ),
        in_specs=[pl.BlockSpec(memory_space=pltpu.HBM)] * len(args),
        out_specs=(vmem,) * 5,
        scratch_shapes=[pltpu.VMEM(a.shape, a.dtype) for a in args[1:]]
        + [pltpu.SemaphoreType.DMA((len(args),))],
        compiler_params=room(4),
    )(*[pltpu.with_memory_space_constraint(a, pltpu.HBM) for a in args])
    plane = pl.pallas_call(
        functools.partial(plane_kernel, trials),
        out_shape=tiled(spans * past),
        in_specs=[vmem] * 5,
        out_specs=vmem,
        scratch_shapes=[
            pltpu.VMEM((rows, spans * span), filterbank.dtype),
            pltpu.VMEM((rows * spans * past, LANES), jnp.float32),
        ],
        compiler_params=room(6),
    )(own, other, shifts, gain, band)
    for level in range(cross_levels):
        last = level == cross_levels - 1
        mask = spans << level | 1
        there = lax.ppermute(plane, ("sub", "tm"), [(i, i ^ mask) for i in range(subs * spans)])
        scale = 1.0 / math.sqrt(rows * subs) if last else None
        plane = call(
            functools.partial(merge_kernel, level, scale),
            out_shape=(tiled(past),) * 2 if last else tiled(spans * past),
            in_specs=[vmem] * 3,
            out_specs=(vmem,) * 2 if last else vmem,
        )(plane, there, steps)
    keep, send = plane
    return call(
        functools.partial(last_kernel, cross_levels),
        out_shape=jax.ShapeDtypeStruct((trials, span), jnp.float32),
        in_specs=[vmem] * 2,
        out_specs=vmem,
    )(keep, lax.ppermute(send, "tm", swap))


def solution(mesh):
    return jax.shard_map(
        shards,
        mesh=mesh,
        in_specs=(P(("beam", "sub"), "tm"), P(("beam", "sub")), P(None, "sub"), P(None, "sub")),
        out_specs=P(("beam", "sub"), "tm"),
        check_vma=False,
    )
```

profile of v0, /device:TPU:0, one launch (start us, length us, event | category | flops | bytes accessed | tf_op | source)
XLA Modules:
  0.0 16.9 jit_solution(8258872430106052774)
XLA Ops:
  0.0 0.5 %collective-permute-start = (bf16[128,512]{1,0:T(8,128)(2,1)}, bf16[128,512]{1,0:T(8,128)(2,1)S(1)}, u32[]{:S(2)}, u32[]{:S(2)}) collective-permute-start(bf16[128,512]{1,0:T(8,128)(2,1)} %refs_0_.1), channel_id=1, source_target_pairs={{0,1},{1,0},{2,3},{3,2},{4,5},{5,4},{6,7},{7,6},{8,9},{9,8},{10,11... | collective-permute-start | bytes 393224 | tf_op jit(solution)/shard_map/ppermute | solution.py:236
  0.5 1.0 %shard_map.46 = (bf16[128,512]{1,0:T(8,128)(2,1)S(1)}, s32[384,128]{1,0:T(8,128)S(1)}, f32[128,128]{1,0:T(8,128)S(1)}, s32[24,128]{1,0:T(8,128)S(1)}, bf16[512,256]{1,0:T(8,128)(2,1)S(1)}) custom-call(bf16[128,512]{1,0:T(8,128)(2,1)} %refs_0_.1, f32[1,128]{1,0:T(1,128)} %bitcast.1, s32[7,128]{1,0:T(8,128)} %refs_2_.1, s32[3,16]{1,0:T(4,128)} %refs_3_.1), custom_call_target="tpu_custom_call" | custom-call | tf_op jit(solution)/shard_map/pallas_call | solution.py:238
  1.4 0.2 %collective-permute-done.other_ref = bf16[128,512]{1,0:T(8,128)(2,1)S(1)} collective-permute-done((bf16[128,512]{1,0:T(8,128)(2,1)}, bf16[128,512]{1,0:T(8,128)(2,1)S(1)}, u32[]{:S(2)}, u32[]{:S(2)}) %collective-permute-start) | collective-permute-done | bytes 131104 | tf_op jit(solution)/shard_map/ppermute | solution.py:236
  1.7 1.0 %shard_map.47.own_ref = f32[64,128]{1,0:T(8,128)S(1)} custom-call(bf16[128,512]{1,0:T(8,128)(2,1)S(1)} %get-tuple-element.12.own_ref, bf16[128,512]{1,0:T(8,128)(2,1)S(1)} %collective-permute-done.other_ref, s32[384,128]{1,0:T(8,128)S(1)} %get-tuple-element.13.shifts_ref, f32[128,128]{1,0:T(8,128)S(1)} %get-tuple-element.14.gain_ref, ...), custom_call_target="tpu_custom_call" | custom-call | tf_op jit(solution)/shard_map/pallas_call | solution.py:253
  2.6 2.7 %collective-permute-start.1 = (f32[64,128]{1,0:T(8,128)S(1)}, f32[64,128]{1,0:T(8,128)S(1)}, u32[]{:S(2)}, u32[]{:S(2)}) collective-permute-start(f32[64,128]{1,0:T(8,128)S(1)} %shard_map.47.own_ref), channel_id=1, source_target_pairs={{0,3},{1,2},{2,1},{3,0},{4,7},{5,6},{6,5},{7,4},{8,11},{9,10},{10,... | collective-permute-start | bytes 98312 | tf_op jit(solution)/shard_map/ppermute | solution.py:267
  5.3 1.6 %collective-permute-done.1.there_ref = f32[64,128]{1,0:T(8,128)S(1)} collective-permute-done((f32[64,128]{1,0:T(8,128)S(1)}, f32[64,128]{1,0:T(8,128)S(1)}, u32[]{:S(2)}, u32[]{:S(2)}) %collective-permute-start.1) | collective-permute-done | bytes 32800 | tf_op jit(solution)/shard_map/ppermute | solution.py:267
  6.9 0.1 shard_map.48.own_ref
  7.0 1.9 %collective-permute-start.2 = (f32[64,128]{1,0:T(8,128)S(1)}, f32[64,128]{1,0:T(8,128)S(1)}, u32[]{:S(2)}, u32[]{:S(2)}) collective-permute-start(f32[64,128]{1,0:T(8,128)S(1)} %shard_map.48.own_ref), channel_id=1, source_target_pairs={{0,5},{1,4},{2,7},{3,6},{4,1},{5,0},{6,3},{7,2},{8,13},{9,12},{10,... | collective-permute-start | bytes 98312 | tf_op jit(solution)/shard_map/ppermute | solution.py:267
  8.8 1.6 %collective-permute-done.2.there_ref = f32[64,128]{1,0:T(8,128)S(1)} collective-permute-done((f32[64,128]{1,0:T(8,128)S(1)}, f32[64,128]{1,0:T(8,128)S(1)}, u32[]{:S(2)}, u32[]{:S(2)}) %collective-permute-start.2) | collective-permute-done | bytes 32800 | tf_op jit(solution)/shard_map/ppermute | solution.py:267
  10.4 0.1 shard_map.49.own_ref
  10.5 2.8 %collective-permute-start.3 = (f32[64,128]{1,0:T(8,128)S(1)}, f32[64,128]{1,0:T(8,128)S(1)}, u32[]{:S(2)}, u32[]{:S(2)}) collective-permute-start(f32[64,128]{1,0:T(8,128)S(1)} %shard_map.49.own_ref), channel_id=1, source_target_pairs={{0,9},{1,8},{2,11},{3,10},{4,13},{5,12},{6,15},{7,14},{8,1},{9,0},... | collective-permute-start | bytes 98312 | tf_op jit(solution)/shard_map/ppermute | solution.py:267
  13.3 1.6 %collective-permute-done.3.there_ref = f32[64,128]{1,0:T(8,128)S(1)} collective-permute-done((f32[64,128]{1,0:T(8,128)S(1)}, f32[64,128]{1,0:T(8,128)S(1)}, u32[]{:S(2)}, u32[]{:S(2)}) %collective-permute-start.3) | collective-permute-done | bytes 32800 | tf_op jit(solution)/shard_map/ppermute | solution.py:267
  14.9 0.1 shard_map.50
  15.0 0.4 %collective-permute-start.4 = (f32[32,128]{1,0:T(8,128)S(1)}, f32[32,128]{1,0:T(8,128)S(1)}, u32[]{:S(2)}, u32[]{:S(2)}) collective-permute-start(f32[32,128]{1,0:T(8,128)S(1)} %get-tuple-element.18), channel_id=1, source_target_pairs={{0,1},{1,0},{2,3},{3,2},{4,5},{5,4},{6,7},{7,6},{8,9},{9,8},{10,11... | collective-permute-start | bytes 49160 | tf_op jit(solution)/shard_map/ppermute | solution.py:281
  15.4 0.8 %collective-permute-done.4.there_ref = f32[32,128]{1,0:T(8,128)S(1)} collective-permute-done((f32[32,128]{1,0:T(8,128)S(1)}, f32[32,128]{1,0:T(8,128)S(1)}, u32[]{:S(2)}, u32[]{:S(2)}) %collective-permute-start.4) | collective-permute-done | bytes 16416 | tf_op jit(solution)/shard_map/ppermute | solution.py:281
  16.2 0.6 %shard_map.51 = f32[16,512]{1,0:T(8,128)} custom-call(f32[32,128]{1,0:T(8,128)S(1)} %get-tuple-element.17.keep_ref, f32[32,128]{1,0:T(8,128)S(1)} %collective-permute-done.4.there_ref), custom_call_target="tpu_custom_call" | custom-call | tf_op jit(solution)/shard_map/pallas_call | solution.py:276
Async XLA Ops:
  0.0 1.6 %collective-permute-start = (bf16[128,512]{1,0:T(8,128)(2,1)}, bf16[128,512]{1,0:T(8,128)(2,1)S(1)}, u32[]{:S(2)}, u32[]{:S(2)}) collective-permute-start(bf16[128,512]{1,0:T(8,128)(2,1)} %refs_0_.1), channel_id=1, source_target_pairs={{0,1},{1,0},{2,3},{3,2},{4,5},{5,4},{6,7},{7,6},{8,9},{9,8},{10,11... | collective-permute-start | bytes 393224 | tf_op jit(solution)/shard_map/ppermute | solution.py:236
  2.6 4.3 %collective-permute-start.1 = (f32[64,128]{1,0:T(8,128)S(1)}, f32[64,128]{1,0:T(8,128)S(1)}, u32[]{:S(2)}, u32[]{:S(2)}) collective-permute-start(f32[64,128]{1,0:T(8,128)S(1)} %shard_map.47.own_ref), channel_id=1, source_target_pairs={{0,3},{1,2},{2,1},{3,0},{4,7},{5,6},{6,5},{7,4},{8,11},{9,10},{10,... | collective-permute-start | bytes 98312 | tf_op jit(solution)/shard_map/ppermute | solution.py:267
  7.0 3.5 %collective-permute-start.2 = (f32[64,128]{1,0:T(8,128)S(1)}, f32[64,128]{1,0:T(8,128)S(1)}, u32[]{:S(2)}, u32[]{:S(2)}) collective-permute-start(f32[64,128]{1,0:T(8,128)S(1)} %shard_map.48.own_ref), channel_id=1, source_target_pairs={{0,5},{1,4},{2,7},{3,6},{4,1},{5,0},{6,3},{7,2},{8,13},{9,12},{10,... | collective-permute-start | bytes 98312 | tf_op jit(solution)/shard_map/ppermute | solution.py:267
  10.5 4.4 %collective-permute-start.3 = (f32[64,128]{1,0:T(8,128)S(1)}, f32[64,128]{1,0:T(8,128)S(1)}, u32[]{:S(2)}, u32[]{:S(2)}) collective-permute-start(f32[64,128]{1,0:T(8,128)S(1)} %shard_map.49.own_ref), channel_id=1, source_target_pairs={{0,9},{1,8},{2,11},{3,10},{4,13},{5,12},{6,15},{7,14},{8,1},{9,0},... | collective-permute-start | bytes 98312 | tf_op jit(solution)/shard_map/ppermute | solution.py:267
  15.0 1.3 %collective-permute-start.4 = (f32[32,128]{1,0:T(8,128)S(1)}, f32[32,128]{1,0:T(8,128)S(1)}, u32[]{:S(2)}, u32[]{:S(2)}) collective-permute-start(f32[32,128]{1,0:T(8,128)S(1)} %get-tuple-element.18), channel_id=1, source_target_pairs={{0,1},{1,0},{2,3},{3,2},{4,5},{5,4},{6,7},{7,6},{8,9},{9,8},{10,11... | collective-permute-start | bytes 49160 | tf_op jit(solution)/shard_map/ppermute | solution.py:281
where the time goes:
time: 17.1 us; the launch traced here: 16.9 us
  starting transfers between devices  8.17 us (48%)
  waiting for transfers between devices  5.84 us (34%)
  Pallas kernels  2.83 us (17%)
    ppermute x3, starting transfers between devices, shards(): lax.ppermute(plane, ('sub', 'tm'), [(i, i ^ mask) for i in range(subs * s...  7.3 us
    ppermute x3, waiting for transfers between devices, shards(): lax.ppermute(plane, ('sub', 'tm'), [(i, i ^ mask) for i in range(subs * s...  4.8 us
    pallas_call x1, Pallas kernels, shards(): pl.pallas_call(table_kernel, out_shape=(jax.ShapeDtypeStruct(filterbank.s...  0.99 us
    pallas_call x1, Pallas kernels, shards(): pl.pallas_call(functools.partial(plane_kernel, trials), out_shape=tiled(s...  0.97 us
    ppermute x1, waiting for transfers between devices, shards(): lax.ppermute(send, 'tm', swap)  0.84 us
    pallas_call x1, Pallas kernels, shards(): call(functools.partial(last_kernel, cross_levels), out_shape=jax.ShapeDty...  0.63 us
    ppermute x1, starting transfers between devices, shards(): other = lax.ppermute(filterbank, 'tm', swap)  0.45 us
    ppermute x1, starting transfers between devices, shards(): lax.ppermute(send, 'tm', swap)  0.42 us
  transfers between devices with their start and end apart: 5, of which 5 were waited for; matrix products, arithmetic and copies ran while one was open for 0% of the time, Pallas kernels for 6%

commit v1 on v0

--- a/solution.py
+++ b/solution.py
@@ -12,6 +12,7 @@
 SUBLANES = 8
 WINDOW = 31
 HALF = WINDOW // 2
+CODE_TOP = 32000.0
 
 
 def iota(shape, axis):
@@ -183,12 +184,29 @@
     return ref[block * SUBLANES : (block + 1) * SUBLANES, :]
 
 
+def coded(tile):
+    top = jnp.max(jnp.abs(tile), axis=1, keepdims=True)
+    exponent = jnp.ceil(jnp.log(jnp.maximum(top, 2.0**-100)) * (1.0 / math.log(2.0)))
+    return jnp.round(tile * (jnp.exp2(-exponent) * CODE_TOP)).astype(jnp.int32), exponent.astype(jnp.int32)
+
+
 def merge_kernel(level, scale, own_ref, there_ref, steps_ref, out_ref, send_ref=None):
     is_upper = lax.axis_index("sub") >> level & 1 == 1
     blocks = own_ref.shape[0] // SUBLANES
+    pair = 2 * SUBLANES
+    if there_ref.dtype == jnp.int16:
+        exponents = there_ref[blocks * SUBLANES :, :].astype(jnp.int32)[:SUBLANES]
     lower, upper = [], []
     for block in range(blocks):
-        own, there = tile_of(own_ref, block), tile_of(there_ref, block)
+        own = tile_of(own_ref, block)
+        if there_ref.dtype == jnp.int16:
+            at_row = block // 2 * pair
+            there = there_ref[at_row : at_row + pair, :].astype(jnp.int32)
+            there = there[block % 2 * SUBLANES : (block % 2 + 1) * SUBLANES].astype(jnp.float32)
+            exponent = turned(exponents, jnp.full(exponents.shape, block, jnp.int32), 1)
+            there = there * (jnp.exp2(exponent.astype(jnp.float32)) * (1.0 / CODE_TOP))
+        else:
+            there = tile_of(there_ref, block)
         lower.append(jnp.where(is_upper, there, own))
         upper.append(jnp.where(is_upper, own, there))
     moved = later(upper, tile_of(steps_ref, level), blocks)
@@ -196,6 +214,18 @@
     if scale is None:
         for block in range(blocks):
             out_ref[block * SUBLANES : (block + 1) * SUBLANES, :] = new[block]
+        if send_ref is not None:
+            lane = iota((SUBLANES, LANES), 1)
+            notes = jnp.zeros((SUBLANES, LANES), jnp.int32)
+            codes = []
+            for block in range(blocks):
+                code, exponent = coded(new[block])
+                codes.append(code)
+                notes = jnp.where(lane == block, exponent, notes)
+            codes += [notes, notes]
+            for i in range(0, len(codes), 2):
+                both = jnp.concatenate(codes[i : i + 2], axis=0).astype(jnp.int16)
+                send_ref[i * SUBLANES : (i + 2) * SUBLANES, :] = both
         return
     first_span = lax.axis_index("tm") == 0
     past = blocks // 2
@@ -261,18 +291,23 @@
         ],
         compiler_params=room(6),
     )(own, other, shifts, gain, band)
+    sent = plane
     for level in range(cross_levels):
-        last = level == cross_levels - 1
         mask = spans << level | 1
-        there = lax.ppermute(plane, ("sub", "tm"), [(i, i ^ mask) for i in range(subs * spans)])
-        scale = 1.0 / math.sqrt(rows * subs) if last else None
-        plane = call(
+        there = lax.ppermute(sent, ("sub", "tm"), [(i, i ^ mask) for i in range(subs * spans)])
+        scale, shapes = None, (tiled(spans * past),)
+        if level == cross_levels - 2:
+            shapes += (tiled(spans * past + 2, jnp.int16),)
+        elif level == cross_levels - 1:
+            scale, shapes = 1.0 / math.sqrt(rows * subs), (tiled(past),) * 2
+        plane, *more = call(
             functools.partial(merge_kernel, level, scale),
-            out_shape=(tiled(past),) * 2 if last else tiled(spans * past),
+            out_shape=shapes,
             in_specs=[vmem] * 3,
-            out_specs=(vmem,) * 2 if last else vmem,
+            out_specs=(vmem,) * len(shapes),
         )(plane, there, steps)
-    keep, send = plane
+        sent = more[0] if more else plane
+    keep, send = plane, sent
     return call(
         functools.partial(last_kernel, cross_levels),
         out_shape=jax.ShapeDtypeStruct((trials, span), jnp.float32),

time: 17.1 us -> 17.1 us (level)
  no operation moved by 1% of the time
where the time goes in v1:
time: 17.1 us; the launch traced here: 17 us
  starting transfers between devices  8.22 us (48%)
  waiting for transfers between devices  5.73 us (34%)
  Pallas kernels  3 us (18%)
    ppermute x3, starting transfers between devices, shards(): lax.ppermute(sent, ('sub', 'tm'), [(i, i ^ mask) for i in range(subs * sp...  7.36 us
    ppermute x3, waiting for transfers between devices, shards(): lax.ppermute(sent, ('sub', 'tm'), [(i, i ^ mask) for i in range(subs * sp...  4.68 us
    pallas_call x1, Pallas kernels, shards(): pl.pallas_call(table_kernel, out_shape=(jax.ShapeDtypeStruct(filterbank.s...  0.99 us
    pallas_call x1, Pallas kernels, shards(): pl.pallas_call(functools.partial(plane_kernel, trials), out_shape=tiled(s...  0.97 us
    ppermute x1, waiting for transfers between devices, shards(): lax.ppermute(send, 'tm', swap)  0.84 us
    pallas_call x1, Pallas kernels, shards(): call(functools.partial(last_kernel, cross_levels), out_shape=jax.ShapeDty...  0.63 us
    ppermute x1, starting transfers between devices, shards(): other = lax.ppermute(filterbank, 'tm', swap)  0.45 us
    pallas_call x3, Pallas kernels, shards(): call(functools.partial(merge_kernel, level, scale), out_shape=shapes, in_...  0.42 us
  transfers between devices with their start and end apart: 5, of which 5 were waited for; matrix products, arithmetic and copies ran while one was open for 0% of the time, Pallas kernels for 6%

profile of v1, /device:TPU:0, one launch (start us, length us, event | category | flops | bytes accessed | tf_op | source)
XLA Modules:
  0.0 17.0 jit_solution(14855996269757919049)
XLA Ops:
  0.0 0.5 %collective-permute-start = (bf16[128,512]{1,0:T(8,128)(2,1)}, bf16[128,512]{1,0:T(8,128)(2,1)S(1)}, u32[]{:S(2)}, u32[]{:S(2)}) collective-permute-start(bf16[128,512]{1,0:T(8,128)(2,1)} %refs_0_.1), channel_id=1, source_target_pairs={{0,1},{1,0},{2,3},{3,2},{4,5},{5,4},{6,7},{7,6},{8,9},{9,8},{10,11... | collective-permute-start | bytes 393224 | tf_op jit(solution)/shard_map/ppermute | solution.py:266
  0.5 1.0 %shard_map.46 = (bf16[128,512]{1,0:T(8,128)(2,1)S(1)}, s32[384,128]{1,0:T(8,128)S(1)}, f32[128,128]{1,0:T(8,128)S(1)}, s32[24,128]{1,0:T(8,128)S(1)}, bf16[512,256]{1,0:T(8,128)(2,1)S(1)}) custom-call(bf16[128,512]{1,0:T(8,128)(2,1)} %refs_0_.1, f32[1,128]{1,0:T(1,128)} %bitcast.1, s32[7,128]{1,0:T(8,128)} %refs_2_.1, s32[3,16]{1,0:T(4,128)} %refs_3_.1), custom_call_target="tpu_custom_call" | custom-call | tf_op jit(solution)/shard_map/pallas_call | solution.py:268
  1.4 0.2 %collective-permute-done.other_ref = bf16[128,512]{1,0:T(8,128)(2,1)S(1)} collective-permute-done((bf16[128,512]{1,0:T(8,128)(2,1)}, bf16[128,512]{1,0:T(8,128)(2,1)S(1)}, u32[]{:S(2)}, u32[]{:S(2)}) %collective-permute-start) | collective-permute-done | bytes 131104 | tf_op jit(solution)/shard_map/ppermute | solution.py:266
  1.7 1.0 %shard_map.47.own_ref = f32[64,128]{1,0:T(8,128)S(1)} custom-call(bf16[128,512]{1,0:T(8,128)(2,1)S(1)} %get-tuple-element.14.own_ref, bf16[128,512]{1,0:T(8,128)(2,1)S(1)} %collective-permute-done.other_ref, s32[384,128]{1,0:T(8,128)S(1)} %get-tuple-element.15.shifts_ref, f32[128,128]{1,0:T(8,128)S(1)} %get-tuple-element.16.gain_ref, ...), custom_call_target="tpu_custom_call" | custom-call | tf_op jit(solution)/shard_map/pallas_call | solution.py:283
  2.6 2.7 %collective-permute-start.1 = (f32[64,128]{1,0:T(8,128)S(1)}, f32[64,128]{1,0:T(8,128)S(1)}, u32[]{:S(2)}, u32[]{:S(2)}) collective-permute-start(f32[64,128]{1,0:T(8,128)S(1)} %shard_map.47.own_ref), channel_id=1, source_target_pairs={{0,3},{1,2},{2,1},{3,0},{4,7},{5,6},{6,5},{7,4},{8,11},{9,10},{10,... | collective-permute-start | bytes 98312 | tf_op jit(solution)/shard_map/ppermute | solution.py:297
  5.3 1.6 %collective-permute-done.1.there_ref = f32[64,128]{1,0:T(8,128)S(1)} collective-permute-done((f32[64,128]{1,0:T(8,128)S(1)}, f32[64,128]{1,0:T(8,128)S(1)}, u32[]{:S(2)}, u32[]{:S(2)}) %collective-permute-start.1) | collective-permute-done | bytes 32800 | tf_op jit(solution)/shard_map/ppermute | solution.py:297
  6.9 0.1 shard_map.48.own_ref
  7.0 1.9 %collective-permute-start.2 = (f32[64,128]{1,0:T(8,128)S(1)}, f32[64,128]{1,0:T(8,128)S(1)}, u32[]{:S(2)}, u32[]{:S(2)}) collective-permute-start(f32[64,128]{1,0:T(8,128)S(1)} %shard_map.48.own_ref), channel_id=1, source_target_pairs={{0,5},{1,4},{2,7},{3,6},{4,1},{5,0},{6,3},{7,2},{8,13},{9,12},{10,... | collective-permute-start | bytes 98312 | tf_op jit(solution)/shard_map/ppermute | solution.py:297
  8.8 1.6 %collective-permute-done.2.there_ref = f32[64,128]{1,0:T(8,128)S(1)} collective-permute-done((f32[64,128]{1,0:T(8,128)S(1)}, f32[64,128]{1,0:T(8,128)S(1)}, u32[]{:S(2)}, u32[]{:S(2)}) %collective-permute-start.2) | collective-permute-done | bytes 32800 | tf_op jit(solution)/shard_map/ppermute | solution.py:297
  10.4 0.2 %shard_map.49 = (f32[64,128]{1,0:T(8,128)S(1)}, s16[80,128]{1,0:T(8,128)(2,1)S(1)}) custom-call(f32[64,128]{1,0:T(8,128)S(1)} %shard_map.48.own_ref, f32[64,128]{1,0:T(8,128)S(1)} %collective-permute-done.2.there_ref, s32[24,128]{1,0:T(8,128)S(1)} %get-tuple-element.18.steps_ref), custom_call_target="tpu_custom_call" | custom-call | tf_op jit(solution)/shard_map/pallas_call | solution.py:303
  10.6 2.8 %collective-permute-start.3 = (s16[80,128]{1,0:T(8,128)(2,1)S(1)}, s16[80,128]{1,0:T(8,128)(2,1)S(1)}, u32[]{:S(2)}, u32[]{:S(2)}) collective-permute-start(s16[80,128]{1,0:T(8,128)(2,1)S(1)} %get-tuple-element.20), channel_id=1, source_target_pairs={{0,9},{1,8},{2,11},{3,10},{4,13},{5,12},{6,15},{7,14},{8,1},{9,0},... | collective-permute-start | bytes 61448 | tf_op jit(solution)/shard_map/ppermute | solution.py:297
  13.5 1.5 %collective-permute-done.3.there_ref = s16[80,128]{1,0:T(8,128)(2,1)S(1)} collective-permute-done((s16[80,128]{1,0:T(8,128)(2,1)S(1)}, s16[80,128]{1,0:T(8,128)(2,1)S(1)}, u32[]{:S(2)}, u32[]{:S(2)}) %collective-permute-start.3) | collective-permute-done | bytes 20512 | tf_op jit(solution)/shard_map/ppermute | solution.py:297
  14.9 0.2 shard_map.50
  15.1 0.4 %collective-permute-start.4 = (f32[32,128]{1,0:T(8,128)S(1)}, f32[32,128]{1,0:T(8,128)S(1)}, u32[]{:S(2)}, u32[]{:S(2)}) collective-permute-start(f32[32,128]{1,0:T(8,128)S(1)} %get-tuple-element.22), channel_id=1, source_target_pairs={{0,1},{1,0},{2,3},{3,2},{4,5},{5,4},{6,7},{7,6},{8,9},{9,8},{10,11... | collective-permute-start | bytes 49160 | tf_op jit(solution)/shard_map/ppermute | solution.py:316
  15.5 0.8 %collective-permute-done.4.there_ref = f32[32,128]{1,0:T(8,128)S(1)} collective-permute-done((f32[32,128]{1,0:T(8,128)S(1)}, f32[32,128]{1,0:T(8,128)S(1)}, u32[]{:S(2)}, u32[]{:S(2)}) %collective-permute-start.4) | collective-permute-done | bytes 16416 | tf_op jit(solution)/shard_map/ppermute | solution.py:316
  16.4 0.6 %shard_map.51 = f32[16,512]{1,0:T(8,128)} custom-call(f32[32,128]{1,0:T(8,128)S(1)} %get-tuple-element.21.keep_ref, f32[32,128]{1,0:T(8,128)S(1)} %collective-permute-done.4.there_ref), custom_call_target="tpu_custom_call" | custom-call | tf_op jit(solution)/shard_map/pallas_call | solution.py:311
Async XLA Ops:
  0.0 1.6 %collective-permute-start = (bf16[128,512]{1,0:T(8,128)(2,1)}, bf16[128,512]{1,0:T(8,128)(2,1)S(1)}, u32[]{:S(2)}, u32[]{:S(2)}) collective-permute-start(bf16[128,512]{1,0:T(8,128)(2,1)} %refs_0_.1), channel_id=1, source_target_pairs={{0,1},{1,0},{2,3},{3,2},{4,5},{5,4},{6,7},{7,6},{8,9},{9,8},{10,11... | collective-permute-start | bytes 393224 | tf_op jit(solution)/shard_map/ppermute | solution.py:266
  2.6 4.3 %collective-permute-start.1 = (f32[64,128]{1,0:T(8,128)S(1)}, f32[64,128]{1,0:T(8,128)S(1)}, u32[]{:S(2)}, u32[]{:S(2)}) collective-permute-start(f32[64,128]{1,0:T(8,128)S(1)} %shard_map.47.own_ref), channel_id=1, source_target_pairs={{0,3},{1,2},{2,1},{3,0},{4,7},{5,6},{6,5},{7,4},{8,11},{9,10},{10,... | collective-permute-start | bytes 98312 | tf_op jit(solution)/shard_map/ppermute | solution.py:297
  7.0 3.5 %collective-permute-start.2 = (f32[64,128]{1,0:T(8,128)S(1)}, f32[64,128]{1,0:T(8,128)S(1)}, u32[]{:S(2)}, u32[]{:S(2)}) collective-permute-start(f32[64,128]{1,0:T(8,128)S(1)} %shard_map.48.own_ref), channel_id=1, source_target_pairs={{0,5},{1,4},{2,7},{3,6},{4,1},{5,0},{6,3},{7,2},{8,13},{9,12},{10,... | collective-permute-start | bytes 98312 | tf_op jit(solution)/shard_map/ppermute | solution.py:297
  10.6 4.3 %collective-permute-start.3 = (s16[80,128]{1,0:T(8,128)(2,1)S(1)}, s16[80,128]{1,0:T(8,128)(2,1)S(1)}, u32[]{:S(2)}, u32[]{:S(2)}) collective-permute-start(s16[80,128]{1,0:T(8,128)(2,1)S(1)} %get-tuple-element.20), channel_id=1, source_target_pairs={{0,9},{1,8},{2,11},{3,10},{4,13},{5,12},{6,15},{7,14},{8,1},{9,0},... | collective-permute-start | bytes 61448 | tf_op jit(solution)/shard_map/ppermute | solution.py:297
  15.1 1.2 %collective-permute-start.4 = (f32[32,128]{1,0:T(8,128)S(1)}, f32[32,128]{1,0:T(8,128)S(1)}, u32[]{:S(2)}, u32[]{:S(2)}) collective-permute-start(f32[32,128]{1,0:T(8,128)S(1)} %get-tuple-element.22), channel_id=1, source_target_pairs={{0,1},{1,0},{2,3},{3,2},{4,5},{5,4},{6,7},{7,6},{8,9},{9,8},{10,11... | collective-permute-start | bytes 49160 | tf_op jit(solution)/shard_map/ppermute | solution.py:316

commit v2 on v0

--- a/solution.py
+++ b/solution.py
@@ -53,8 +53,8 @@
 
 def table_kernel(*refs):
     fb_ref, *sources = refs[:4]
-    own_ref, shifts_ref, gain_ref, steps_ref, band_ref = refs[4:9]
-    held, sems = refs[9:12], refs[12]
+    own_ref, own_level_ref, shifts_ref, gain_ref, steps_ref, band_ref = refs[4:10]
+    held, sems = refs[10:13], refs[13]
     copies = [
         pltpu.make_async_copy(a, b, sems.at[i])
         for i, (a, b) in enumerate(zip([*sources, fb_ref], [*held, own_ref]))
@@ -119,40 +119,51 @@
         step = jnp.broadcast_to(step, (SUBLANES, LANES)).astype(jnp.int32)
         steps_ref[l * SUBLANES : (l + 1) * SUBLANES, :] = step
     copies[-1].wait()
-
-
-def plane_kernel(trials, own_ref, other_ref, shifts_ref, gain_ref, band_ref, out_ref, whole_ref, level_ref):
-    rows, span = own_ref.shape
-    grow = trials.bit_length() - 1
-    columns = whole_ref.shape[1]
-    blocks = columns // LANES
-    first_span = lax.axis_index("tm") == 0
-
-    @pl.when(first_span)
-    def _():
-        whole_ref[:, :span] = own_ref[...]
-        whole_ref[:, span:] = other_ref[...]
-
-    @pl.when(jnp.logical_not(first_span))
-    def _():
-        whole_ref[:, :span] = other_ref[...]
-        whole_ref[:, span:] = own_ref[...]
-
+    window_sums(own_ref, band_ref, own_level_ref)
+
+
+def window_sums(samples_ref, band_ref, level_ref):
+    rows = samples_ref.shape[0]
+    blocks = samples_ref.shape[1] // LANES
     for block in range(0, blocks, 2):
         low, high = max(block - 1, 0), min(block + 3, blocks)
         part = band_ref[(low - block + 1) * LANES : (high - block + 1) * LANES, :]
         got = jnp.dot(
-            whole_ref[:, low * LANES : high * LANES], part, preferred_element_type=jnp.float32
+            samples_ref[:, low * LANES : high * LANES], part, preferred_element_type=jnp.float32
         )
         level_ref[block * rows : (block + 1) * rows, :] = got[:, :LANES]
         level_ref[(block + 1) * rows : (block + 2) * rows, :] = got[:, LANES:]
 
+
+def plane_kernel(trials, *refs):
+    own_ref, other_ref, own_level_ref, shifts_ref, gain_ref, band_ref = refs[:6]
+    out_ref, other_level_ref, seam_ref = refs[6:]
+    rows, span = own_ref.shape
+    grow = trials.bit_length() - 1
+    per_span = span // LANES
+    blocks = 2 * per_span
+    first_span = lax.axis_index("tm") == 0
+    window_sums(other_ref, band_ref, other_level_ref)
+
+    own_early, own_late = own_ref[:, span - LANES :], own_ref[:, :LANES]
+    other_early, other_late = other_ref[:, span - LANES :], other_ref[:, :LANES]
+    early = jnp.where(first_span, own_early, other_early)
+    late = jnp.where(first_span, other_late, own_late)
+    after, before = band_ref[3 * LANES :, LANES:], band_ref[:LANES, :LANES]
+    seam_ref[:rows, :] = jnp.dot(late, after, preferred_element_type=jnp.float32)
+    seam_ref[rows:, :] = jnp.dot(early, before, preferred_element_type=jnp.float32)
+
     bands = []
     for e in range(trials):
         scale = gain_ref[e * SUBLANES : (e + 1) * SUBLANES, :]
-        bands.append(
-            [level_ref[pl.ds(block * rows + e, SUBLANES, stride=trials), :] * scale for block in range(blocks)]
-        )
+        rows_of = lambda ref, block: ref[pl.ds(block * rows + e, SUBLANES, stride=trials), :]
+        own = [rows_of(own_level_ref, block) for block in range(per_span)]
+        other = [rows_of(other_level_ref, block) for block in range(per_span)]
+        tiles = [jnp.where(first_span, a, b) for a, b in zip(own, other)]
+        tiles += [jnp.where(first_span, b, a) for a, b in zip(own, other)]
+        tiles[per_span - 1] += rows_of(seam_ref, 0)
+        tiles[per_span] += rows_of(seam_ref, 1)
+        bands.append([tile * scale for tile in tiles])
     plane = [bands]
 
     def merged(low, high, at_row):
@@ -235,17 +246,18 @@
     swap = [(0, 1), (1, 0)]
     other = lax.ppermute(filterbank, "tm", swap)
     args = (filterbank, bandpass[None, :], local_delays, cross_delays)
-    own, shifts, gain, steps, band = pl.pallas_call(
+    own, own_level, shifts, gain, steps, band = pl.pallas_call(
         table_kernel,
         out_shape=(
             jax.ShapeDtypeStruct(filterbank.shape, filterbank.dtype),
+            tiled(past * trials),
             tiled((grow + 2) // 2 * trials, jnp.int32),
             tiled(trials),
             tiled(cross_levels, jnp.int32),
             jax.ShapeDtypeStruct((4 * LANES, 2 * LANES), jnp.bfloat16),
         ),
         in_specs=[pl.BlockSpec(memory_space=pltpu.HBM)] * len(args),
-        out_specs=(vmem,) * 5,
+        out_specs=(vmem,) * 6,
         scratch_shapes=[pltpu.VMEM(a.shape, a.dtype) for a in args[1:]]
         + [pltpu.SemaphoreType.DMA((len(args),))],
         compiler_params=room(4),
@@ -253,14 +265,14 @@
     plane = pl.pallas_call(
         functools.partial(plane_kernel, trials),
         out_shape=tiled(spans * past),
-        in_specs=[vmem] * 5,
+        in_specs=[vmem] * 6,
         out_specs=vmem,
         scratch_shapes=[
-            pltpu.VMEM((rows, spans * span), filterbank.dtype),
-            pltpu.VMEM((rows * spans * past, LANES), jnp.float32),
+            pltpu.VMEM((rows * past, LANES), jnp.float32),
+            pltpu.VMEM((rows * 2, LANES), jnp.float32),
         ],
         compiler_params=room(6),
-    )(own, other, shifts, gain, band)
+    )(own, other, own_level, shifts, gain, band)
     for level in range(cross_levels):
         last = level == cross_levels - 1
         mask = spans << level | 1

time: 17.1 us -> 17 us (level)
  Pallas kernels: 2.83 us -> 3.08 us
    pallas_call x1, Pallas kernels: 0.99 us -> 1.27 us  [shards(): pl.pallas_call(table_kernel, out_shape=(jax.ShapeDtypeStruct(filterbank.s...]
    ppermute x1, waiting for transfers between devices: 0.2 us -> 0.01 us  [shards(): other = lax.ppermute(filterbank, 'tm', swap)]
  transfers between devices with their start and end apart: 5 -> 5, of which waited for: 5 -> 4; matrix products, arithmetic and copies ran while one was open for 0% -> 0% of each run, Pallas kernels for 6% -> 8%
where the time goes in v2:
time: 17 us; the launch traced here: 16.9 us
  starting transfers between devices  8.04 us (47%)
  waiting for transfers between devices  5.72 us (34%)
  Pallas kernels  3.08 us (18%)
    ppermute x3, starting transfers between devices, shards(): lax.ppermute(plane, ('sub', 'tm'), [(i, i ^ mask) for i in range(subs * s...  7.26 us
    ppermute x3, waiting for transfers between devices, shards(): lax.ppermute(plane, ('sub', 'tm'), [(i, i ^ mask) for i in range(subs * s...  4.8 us
    pallas_call x1, Pallas kernels, shards(): pl.pallas_call(table_kernel, out_shape=(jax.ShapeDtypeStruct(filterbank.s...  1.27 us
    pallas_call x1, Pallas kernels, shards(): pl.pallas_call(functools.partial(plane_kernel, trials), out_shape=tiled(s...  0.93 us
    ppermute x1, waiting for transfers between devices, shards(): lax.ppermute(send, 'tm', swap)  0.92 us
    pallas_call x1, Pallas kernels, shards(): call(functools.partial(last_kernel, cross_levels), out_shape=jax.ShapeDty...  0.63 us
    ppermute x1, starting transfers between devices, shards(): other = lax.ppermute(filterbank, 'tm', swap)  0.45 us
  transfers between devices with their start and end apart: 5, of which 4 were waited for; matrix products, arithmetic and copies ran while one was open for 0% of the time, Pallas kernels for 8%

profile of v2, /device:TPU:0, one launch (start us, length us, event | category | flops | bytes accessed | tf_op | source)
XLA Modules:
  0.0 16.9 jit_solution(14154940882107773133)
XLA Ops:
  0.0 0.5 %collective-permute-start = (bf16[128,512]{1,0:T(8,128)(2,1)}, bf16[128,512]{1,0:T(8,128)(2,1)S(1)}, u32[]{:S(2)}, u32[]{:S(2)}) collective-permute-start(bf16[128,512]{1,0:T(8,128)(2,1)} %refs_0_.1), channel_id=1, source_target_pairs={{0,1},{1,0},{2,3},{3,2},{4,5},{5,4},{6,7},{7,6},{8,9},{9,8},{10,11... | collective-permute-start | bytes 393224 | tf_op jit(solution)/shard_map/ppermute | solution.py:247
  0.5 1.3 %shard_map.46 = (bf16[128,512]{1,0:T(8,128)(2,1)S(1)}, f32[512,128]{1,0:T(8,128)S(1)}, s32[384,128]{1,0:T(8,128)S(1)}, f32[128,128]{1,0:T(8,128)S(1)}, s32[24,12...) custom-call(bf16[128,512]{1,0:T(8,128)(2,1)} %refs_0_.1, f32[1,128]{1,0:T(1,128)} %bitcast.1, s32[7,128]{1,0:T(8,128)} %refs_2_.1, ...), custom_call_target="tpu_custom_call" | custom-call | tf_op jit(solution)/shard_map/pallas_call | solution.py:249
  1.7 0.0 collective-permute-done.refs_1_
  1.7 0.9 %shard_map.47.own_ref = f32[64,128]{1,0:T(8,128)S(1)} custom-call(bf16[128,512]{1,0:T(8,128)(2,1)S(1)} %get-tuple-element.13.refs_0_, bf16[128,512]{1,0:T(8,128)(2,1)S(1)} %collective-permute-done.refs_1_, f32[512,128]{1,0:T(8,128)S(1)} %get-tuple-element.14.refs_2_, s32[384,128]{1,0:T(8,128)S(1)} %get-tuple-element.15.refs_3_, ...), custom_call_target="tpu_custom_call" | custom-call | tf_op jit(solution)/shard_map/pallas_call | solution.py:265
  2.7 2.7 %collective-permute-start.1 = (f32[64,128]{1,0:T(8,128)S(1)}, f32[64,128]{1,0:T(8,128)S(1)}, u32[]{:S(2)}, u32[]{:S(2)}) collective-permute-start(f32[64,128]{1,0:T(8,128)S(1)} %shard_map.47.own_ref), channel_id=1, source_target_pairs={{0,3},{1,2},{2,1},{3,0},{4,7},{5,6},{6,5},{7,4},{8,11},{9,10},{10,... | collective-permute-start | bytes 98312 | tf_op jit(solution)/shard_map/ppermute | solution.py:279
  5.3 1.6 %collective-permute-done.1.there_ref = f32[64,128]{1,0:T(8,128)S(1)} collective-permute-done((f32[64,128]{1,0:T(8,128)S(1)}, f32[64,128]{1,0:T(8,128)S(1)}, u32[]{:S(2)}, u32[]{:S(2)}) %collective-permute-start.1) | collective-permute-done | bytes 32800 | tf_op jit(solution)/shard_map/ppermute | solution.py:279
  6.9 0.1 shard_map.48.own_ref
  7.0 1.8 %collective-permute-start.2 = (f32[64,128]{1,0:T(8,128)S(1)}, f32[64,128]{1,0:T(8,128)S(1)}, u32[]{:S(2)}, u32[]{:S(2)}) collective-permute-start(f32[64,128]{1,0:T(8,128)S(1)} %shard_map.48.own_ref), channel_id=1, source_target_pairs={{0,5},{1,4},{2,7},{3,6},{4,1},{5,0},{6,3},{7,2},{8,13},{9,12},{10,... | collective-permute-start | bytes 98312 | tf_op jit(solution)/shard_map/ppermute | solution.py:279
  8.9 1.6 %collective-permute-done.2.there_ref = f32[64,128]{1,0:T(8,128)S(1)} collective-permute-done((f32[64,128]{1,0:T(8,128)S(1)}, f32[64,128]{1,0:T(8,128)S(1)}, u32[]{:S(2)}, u32[]{:S(2)}) %collective-permute-start.2) | collective-permute-done | bytes 32800 | tf_op jit(solution)/shard_map/ppermute | solution.py:279
  10.5 0.1 shard_map.49.own_ref
  10.5 2.8 %collective-permute-start.3 = (f32[64,128]{1,0:T(8,128)S(1)}, f32[64,128]{1,0:T(8,128)S(1)}, u32[]{:S(2)}, u32[]{:S(2)}) collective-permute-start(f32[64,128]{1,0:T(8,128)S(1)} %shard_map.49.own_ref), channel_id=1, source_target_pairs={{0,9},{1,8},{2,11},{3,10},{4,13},{5,12},{6,15},{7,14},{8,1},{9,0},... | collective-permute-start | bytes 98312 | tf_op jit(solution)/shard_map/ppermute | solution.py:279
  13.3 1.6 %collective-permute-done.3.there_ref = f32[64,128]{1,0:T(8,128)S(1)} collective-permute-done((f32[64,128]{1,0:T(8,128)S(1)}, f32[64,128]{1,0:T(8,128)S(1)}, u32[]{:S(2)}, u32[]{:S(2)}) %collective-permute-start.3) | collective-permute-done | bytes 32800 | tf_op jit(solution)/shard_map/ppermute | solution.py:279
  14.9 0.1 shard_map.50
  15.0 0.3 %collective-permute-start.4 = (f32[32,128]{1,0:T(8,128)S(1)}, f32[32,128]{1,0:T(8,128)S(1)}, u32[]{:S(2)}, u32[]{:S(2)}) collective-permute-start(f32[32,128]{1,0:T(8,128)S(1)} %get-tuple-element.20), channel_id=1, source_target_pairs={{0,1},{1,0},{2,3},{3,2},{4,5},{5,4},{6,7},{7,6},{8,9},{9,8},{10,11... | collective-permute-start | bytes 49160 | tf_op jit(solution)/shard_map/ppermute | solution.py:293
  15.3 0.9 %collective-permute-done.4.there_ref = f32[32,128]{1,0:T(8,128)S(1)} collective-permute-done((f32[32,128]{1,0:T(8,128)S(1)}, f32[32,128]{1,0:T(8,128)S(1)}, u32[]{:S(2)}, u32[]{:S(2)}) %collective-permute-start.4) | collective-permute-done | bytes 16416 | tf_op jit(solution)/shard_map/ppermute | solution.py:293
  16.2 0.6 %shard_map.51 = f32[16,512]{1,0:T(8,128)} custom-call(f32[32,128]{1,0:T(8,128)S(1)} %get-tuple-element.19.keep_ref, f32[32,128]{1,0:T(8,128)S(1)} %collective-permute-done.4.there_ref), custom_call_target="tpu_custom_call" | custom-call | tf_op jit(solution)/shard_map/pallas_call | solution.py:288
Async XLA Ops:
  0.0 1.7 %collective-permute-start = (bf16[128,512]{1,0:T(8,128)(2,1)}, bf16[128,512]{1,0:T(8,128)(2,1)S(1)}, u32[]{:S(2)}, u32[]{:S(2)}) collective-permute-start(bf16[128,512]{1,0:T(8,128)(2,1)} %refs_0_.1), channel_id=1, source_target_pairs={{0,1},{1,0},{2,3},{3,2},{4,5},{5,4},{6,7},{7,6},{8,9},{9,8},{10,11... | collective-permute-start | bytes 393224 | tf_op jit(solution)/shard_map/ppermute | solution.py:247
  2.7 4.3 %collective-permute-start.1 = (f32[64,128]{1,0:T(8,128)S(1)}, f32[64,128]{1,0:T(8,128)S(1)}, u32[]{:S(2)}, u32[]{:S(2)}) collective-permute-start(f32[64,128]{1,0:T(8,128)S(1)} %shard_map.47.own_ref), channel_id=1, source_target_pairs={{0,3},{1,2},{2,1},{3,0},{4,7},{5,6},{6,5},{7,4},{8,11},{9,10},{10,... | collective-permute-start | bytes 98312 | tf_op jit(solution)/shard_map/ppermute | solution.py:279
  7.0 3.4 %collective-permute-start.2 = (f32[64,128]{1,0:T(8,128)S(1)}, f32[64,128]{1,0:T(8,128)S(1)}, u32[]{:S(2)}, u32[]{:S(2)}) collective-permute-start(f32[64,128]{1,0:T(8,128)S(1)} %shard_map.48.own_ref), channel_id=1, source_target_pairs={{0,5},{1,4},{2,7},{3,6},{4,1},{5,0},{6,3},{7,2},{8,13},{9,12},{10,... | collective-permute-start | bytes 98312 | tf_op jit(solution)/shard_map/ppermute | solution.py:279
  10.5 4.4 %collective-permute-start.3 = (f32[64,128]{1,0:T(8,128)S(1)}, f32[64,128]{1,0:T(8,128)S(1)}, u32[]{:S(2)}, u32[]{:S(2)}) collective-permute-start(f32[64,128]{1,0:T(8,128)S(1)} %shard_map.49.own_ref), channel_id=1, source_target_pairs={{0,9},{1,8},{2,11},{3,10},{4,13},{5,12},{6,15},{7,14},{8,1},{9,0},... | collective-permute-start | bytes 98312 | tf_op jit(solution)/shard_map/ppermute | solution.py:279
  15.0 1.2 %collective-permute-start.4 = (f32[32,128]{1,0:T(8,128)S(1)}, f32[32,128]{1,0:T(8,128)S(1)}, u32[]{:S(2)}, u32[]{:S(2)}) collective-permute-start(f32[32,128]{1,0:T(8,128)S(1)} %get-tuple-element.20), channel_id=1, source_target_pairs={{0,1},{1,0},{2,3},{3,2},{4,5},{5,4},{6,7},{7,6},{8,9},{9,8},{10,11... | collective-permute-start | bytes 49160 | tf_op jit(solution)/shard_map/ppermute | solution.py:293

commit v3 on v0

--- a/solution.py
+++ b/solution.py
@@ -138,6 +138,20 @@
         whole_ref[:, :span] = other_ref[...]
         whole_ref[:, span:] = own_ref[...]
 
+    carried = {}
+
+    def moved(tiles, at_row):
+        source = iota((SUBLANES, LANES), 1) - shifts_ref[at_row : at_row + SUBLANES, :]
+        index = source & (LANES - 1)
+        got = []
+        for tile in tiles:
+            spun = turned(tile, index, 1)
+            prior = carried.get(at_row, jnp.zeros((SUBLANES, LANES), jnp.float32))
+            got.append(jnp.where(source >= 0, spun, prior))
+            carried[at_row] = spun
+        return got
+
+    ends = []
     for block in range(0, blocks, 2):
         low, high = max(block - 1, 0), min(block + 3, blocks)
         part = band_ref[(low - block + 1) * LANES : (high - block + 1) * LANES, :]
@@ -146,30 +160,25 @@
         )
         level_ref[block * rows : (block + 1) * rows, :] = got[:, :LANES]
         level_ref[(block + 1) * rows : (block + 2) * rows, :] = got[:, LANES:]
-
-    bands = []
-    for e in range(trials):
-        scale = gain_ref[e * SUBLANES : (e + 1) * SUBLANES, :]
-        bands.append(
-            [level_ref[pl.ds(block * rows + e, SUBLANES, stride=trials), :] * scale for block in range(blocks)]
-        )
-    plane = [bands]
-
-    def merged(low, high, at_row):
-        moved = later(high, shifts_ref[at_row : at_row + SUBLANES, :], blocks)
-        return [a + b for a, b in zip(low, moved)]
-
-    for m in range(grow):
-        old, plane = plane, []
-        for c in range(2 if m else 1):
-            for i, held in enumerate(old):
-                j = c * len(old) + i
-                starts = [m * rows // 2 + ((e << m) + j) * SUBLANES for e in range(len(held) // 2)]
-                plane.append([merged(held[2 * e], held[2 * e + 1], start) for e, start in enumerate(starts)])
-    for j, held in enumerate(plane):
-        at_row = grow * rows // 2 + j * SUBLANES
-        moved = later(held[0], shifts_ref[at_row : at_row + SUBLANES, :], blocks)
-        out_ref[pl.ds(j, SUBLANES, stride=SUBLANES), :] = folded(moved)
+        bands = []
+        for e in range(trials):
+            scale = gain_ref[e * SUBLANES : (e + 1) * SUBLANES, :]
+            starts = [(block + k) * rows + e for k in range(2)]
+            bands.append([level_ref[pl.ds(start, SUBLANES, stride=trials), :] * scale for start in starts])
+        plane = [bands]
+        for m in range(grow):
+            old, plane = plane, []
+            for c in range(2 if m else 1):
+                for i, held in enumerate(old):
+                    j = c * len(old) + i
+                    new = []
+                    for e in range(len(held) // 2):
+                        high_tiles = moved(held[2 * e + 1], m * rows // 2 + ((e << m) + j) * SUBLANES)
+                        new.append([x + y for x, y in zip(held[2 * e], high_tiles)])
+                    plane.append(new)
+        ends.append([moved(held[0], grow * rows // 2 + j * SUBLANES) for j, held in enumerate(plane)])
+    for j in range(SUBLANES):
+        out_ref[pl.ds(j, SUBLANES, stride=SUBLANES), :] = folded([tile for end in ends for tile in end[j]])
 
 
 def row_half(cross_levels):

time: 17.1 us -> 17.3 us (1.012)
  Pallas kernels: 2.83 us -> 3.05 us
    pallas_call x1, Pallas kernels: 0.97 us -> 1.19 us  [shards(): pl.pallas_call(functools.partial(plane_kernel, trials), out_shape=tiled(s...]
where the time goes in v3:
time: 17.3 us; the launch traced here: 17.1 us
  starting transfers between devices  8.17 us (47%)
  waiting for transfers between devices  5.84 us (34%)
  Pallas kernels  3.05 us (18%)
    ppermute x3, starting transfers between devices, shards(): lax.ppermute(plane, ('sub', 'tm'), [(i, i ^ mask) for i in range(subs * s...  7.3 us
    ppermute x3, waiting for transfers between devices, shards(): lax.ppermute(plane, ('sub', 'tm'), [(i, i ^ mask) for i in range(subs * s...  4.8 us
    pallas_call x1, Pallas kernels, shards(): pl.pallas_call(functools.partial(plane_kernel, trials), out_shape=tiled(s...  1.19 us
    pallas_call x1, Pallas kernels, shards(): pl.pallas_call(table_kernel, out_shape=(jax.ShapeDtypeStruct(filterbank.s...  0.99 us
    ppermute x1, waiting for transfers between devices, shards(): lax.ppermute(send, 'tm', swap)  0.84 us
    pallas_call x1, Pallas kernels, shards(): call(functools.partial(last_kernel, cross_levels), out_shape=jax.ShapeDty...  0.63 us
    ppermute x1, starting transfers between devices, shards(): other = lax.ppermute(filterbank, 'tm', swap)  0.45 us
    ppermute x1, starting transfers between devices, shards(): lax.ppermute(send, 'tm', swap)  0.42 us
  transfers between devices with their start and end apart: 5, of which 5 were waited for; matrix products, arithmetic and copies ran while one was open for 0% of the time, Pallas kernels for 6%

profile of v3, /device:TPU:0, one launch (start us, length us, event | category | flops | bytes accessed | tf_op | source)
XLA Modules:
  0.0 17.1 jit_solution(3349925965565654804)
XLA Ops:
  0.0 0.5 %collective-permute-start = (bf16[128,512]{1,0:T(8,128)(2,1)}, bf16[128,512]{1,0:T(8,128)(2,1)S(1)}, u32[]{:S(2)}, u32[]{:S(2)}) collective-permute-start(bf16[128,512]{1,0:T(8,128)(2,1)} %refs_0_.1), channel_id=1, source_target_pairs={{0,1},{1,0},{2,3},{3,2},{4,5},{5,4},{6,7},{7,6},{8,9},{9,8},{10,11... | collective-permute-start | bytes 393224 | tf_op jit(solution)/shard_map/ppermute | solution.py:245
  0.5 1.0 %shard_map.46 = (bf16[128,512]{1,0:T(8,128)(2,1)S(1)}, s32[384,128]{1,0:T(8,128)S(1)}, f32[128,128]{1,0:T(8,128)S(1)}, s32[24,128]{1,0:T(8,128)S(1)}, bf16[512,256]{1,0:T(8,128)(2,1)S(1)}) custom-call(bf16[128,512]{1,0:T(8,128)(2,1)} %refs_0_.1, f32[1,128]{1,0:T(1,128)} %bitcast.1, s32[7,128]{1,0:T(8,128)} %refs_2_.1, s32[3,16]{1,0:T(4,128)} %refs_3_.1), custom_call_target="tpu_custom_call" | custom-call | tf_op jit(solution)/shard_map/pallas_call | solution.py:247
  1.4 0.2 %collective-permute-done.other_ref = bf16[128,512]{1,0:T(8,128)(2,1)S(1)} collective-permute-done((bf16[128,512]{1,0:T(8,128)(2,1)}, bf16[128,512]{1,0:T(8,128)(2,1)S(1)}, u32[]{:S(2)}, u32[]{:S(2)}) %collective-permute-start) | collective-permute-done | bytes 131104 | tf_op jit(solution)/shard_map/ppermute | solution.py:245
  1.7 1.2 %shard_map.47.own_ref = f32[64,128]{1,0:T(8,128)S(1)} custom-call(bf16[128,512]{1,0:T(8,128)(2,1)S(1)} %get-tuple-element.12.own_ref, bf16[128,512]{1,0:T(8,128)(2,1)S(1)} %collective-permute-done.other_ref, s32[384,128]{1,0:T(8,128)S(1)} %get-tuple-element.13.shifts_ref, f32[128,128]{1,0:T(8,128)S(1)} %get-tuple-element.14.gain_ref, ...), custom_call_target="tpu_custom_call" | custom-call | tf_op jit(solution)/shard_map/pallas_call | solution.py:262
  2.8 2.7 %collective-permute-start.1 = (f32[64,128]{1,0:T(8,128)S(1)}, f32[64,128]{1,0:T(8,128)S(1)}, u32[]{:S(2)}, u32[]{:S(2)}) collective-permute-start(f32[64,128]{1,0:T(8,128)S(1)} %shard_map.47.own_ref), channel_id=1, source_target_pairs={{0,3},{1,2},{2,1},{3,0},{4,7},{5,6},{6,5},{7,4},{8,11},{9,10},{10,... | collective-permute-start | bytes 98312 | tf_op jit(solution)/shard_map/ppermute | solution.py:276
  5.5 1.6 %collective-permute-done.1.there_ref = f32[64,128]{1,0:T(8,128)S(1)} collective-permute-done((f32[64,128]{1,0:T(8,128)S(1)}, f32[64,128]{1,0:T(8,128)S(1)}, u32[]{:S(2)}, u32[]{:S(2)}) %collective-permute-start.1) | collective-permute-done | bytes 32800 | tf_op jit(solution)/shard_map/ppermute | solution.py:276
  7.1 0.1 shard_map.48.own_ref
  7.2 1.9 %collective-permute-start.2 = (f32[64,128]{1,0:T(8,128)S(1)}, f32[64,128]{1,0:T(8,128)S(1)}, u32[]{:S(2)}, u32[]{:S(2)}) collective-permute-start(f32[64,128]{1,0:T(8,128)S(1)} %shard_map.48.own_ref), channel_id=1, source_target_pairs={{0,5},{1,4},{2,7},{3,6},{4,1},{5,0},{6,3},{7,2},{8,13},{9,12},{10,... | collective-permute-start | bytes 98312 | tf_op jit(solution)/shard_map/ppermute | solution.py:276
  9.0 1.6 %collective-permute-done.2.there_ref = f32[64,128]{1,0:T(8,128)S(1)} collective-permute-done((f32[64,128]{1,0:T(8,128)S(1)}, f32[64,128]{1,0:T(8,128)S(1)}, u32[]{:S(2)}, u32[]{:S(2)}) %collective-permute-start.2) | collective-permute-done | bytes 32800 | tf_op jit(solution)/shard_map/ppermute | solution.py:276
  10.6 0.1 shard_map.49.own_ref
  10.7 2.8 %collective-permute-start.3 = (f32[64,128]{1,0:T(8,128)S(1)}, f32[64,128]{1,0:T(8,128)S(1)}, u32[]{:S(2)}, u32[]{:S(2)}) collective-permute-start(f32[64,128]{1,0:T(8,128)S(1)} %shard_map.49.own_ref), channel_id=1, source_target_pairs={{0,9},{1,8},{2,11},{3,10},{4,13},{5,12},{6,15},{7,14},{8,1},{9,0},... | collective-permute-start | bytes 98312 | tf_op jit(solution)/shard_map/ppermute | solution.py:276
  13.5 1.6 %collective-permute-done.3.there_ref = f32[64,128]{1,0:T(8,128)S(1)} collective-permute-done((f32[64,128]{1,0:T(8,128)S(1)}, f32[64,128]{1,0:T(8,128)S(1)}, u32[]{:S(2)}, u32[]{:S(2)}) %collective-permute-start.3) | collective-permute-done | bytes 32800 | tf_op jit(solution)/shard_map/ppermute | solution.py:276
  15.1 0.1 shard_map.50
  15.2 0.4 %collective-permute-start.4 = (f32[32,128]{1,0:T(8,128)S(1)}, f32[32,128]{1,0:T(8,128)S(1)}, u32[]{:S(2)}, u32[]{:S(2)}) collective-permute-start(f32[32,128]{1,0:T(8,128)S(1)} %get-tuple-element.18), channel_id=1, source_target_pairs={{0,1},{1,0},{2,3},{3,2},{4,5},{5,4},{6,7},{7,6},{8,9},{9,8},{10,11... | collective-permute-start | bytes 49160 | tf_op jit(solution)/shard_map/ppermute | solution.py:290
  15.6 0.8 %collective-permute-done.4.there_ref = f32[32,128]{1,0:T(8,128)S(1)} collective-permute-done((f32[32,128]{1,0:T(8,128)S(1)}, f32[32,128]{1,0:T(8,128)S(1)}, u32[]{:S(2)}, u32[]{:S(2)}) %collective-permute-start.4) | collective-permute-done | bytes 16416 | tf_op jit(solution)/shard_map/ppermute | solution.py:290
  16.4 0.6 %shard_map.51 = f32[16,512]{1,0:T(8,128)} custom-call(f32[32,128]{1,0:T(8,128)S(1)} %get-tuple-element.17.keep_ref, f32[32,128]{1,0:T(8,128)S(1)} %collective-permute-done.4.there_ref), custom_call_target="tpu_custom_call" | custom-call | tf_op jit(solution)/shard_map/pallas_call | solution.py:285
Async XLA Ops:
  0.0 1.6 %collective-permute-start = (bf16[128,512]{1,0:T(8,128)(2,1)}, bf16[128,512]{1,0:T(8,128)(2,1)S(1)}, u32[]{:S(2)}, u32[]{:S(2)}) collective-permute-start(bf16[128,512]{1,0:T(8,128)(2,1)} %refs_0_.1), channel_id=1, source_target_pairs={{0,1},{1,0},{2,3},{3,2},{4,5},{5,4},{6,7},{7,6},{8,9},{9,8},{10,11... | collective-permute-start | bytes 393224 | tf_op jit(solution)/shard_map/ppermute | solution.py:245
  2.8 4.3 %collective-permute-start.1 = (f32[64,128]{1,0:T(8,128)S(1)}, f32[64,128]{1,0:T(8,128)S(1)}, u32[]{:S(2)}, u32[]{:S(2)}) collective-permute-start(f32[64,128]{1,0:T(8,128)S(1)} %shard_map.47.own_ref), channel_id=1, source_target_pairs={{0,3},{1,2},{2,1},{3,0},{4,7},{5,6},{6,5},{7,4},{8,11},{9,10},{10,... | collective-permute-start | bytes 98312 | tf_op jit(solution)/shard_map/ppermute | solution.py:276
  7.2 3.5 %collective-permute-start.2 = (f32[64,128]{1,0:T(8,128)S(1)}, f32[64,128]{1,0:T(8,128)S(1)}, u32[]{:S(2)}, u32[]{:S(2)}) collective-permute-start(f32[64,128]{1,0:T(8,128)S(1)} %shard_map.48.own_ref), channel_id=1, source_target_pairs={{0,5},{1,4},{2,7},{3,6},{4,1},{5,0},{6,3},{7,2},{8,13},{9,12},{10,... | collective-permute-start | bytes 98312 | tf_op jit(solution)/shard_map/ppermute | solution.py:276
  10.7 4.4 %collective-permute-start.3 = (f32[64,128]{1,0:T(8,128)S(1)}, f32[64,128]{1,0:T(8,128)S(1)}, u32[]{:S(2)}, u32[]{:S(2)}) collective-permute-start(f32[64,128]{1,0:T(8,128)S(1)} %shard_map.49.own_ref), channel_id=1, source_target_pairs={{0,9},{1,8},{2,11},{3,10},{4,13},{5,12},{6,15},{7,14},{8,1},{9,0},... | collective-permute-start | bytes 98312 | tf_op jit(solution)/shard_map/ppermute | solution.py:276
  15.2 1.3 %collective-permute-start.4 = (f32[32,128]{1,0:T(8,128)S(1)}, f32[32,128]{1,0:T(8,128)S(1)}, u32[]{:S(2)}, u32[]{:S(2)}) collective-permute-start(f32[32,128]{1,0:T(8,128)S(1)} %get-tuple-element.18), channel_id=1, source_target_pairs={{0,1},{1,0},{2,3},{3,2},{4,5},{5,4},{6,7},{7,6},{8,9},{9,8},{10,11... | collective-permute-start | bytes 49160 | tf_op jit(solution)/shard_map/ppermute | solution.py:290

commit v4 on v3

--- a/solution.py
+++ b/solution.py
@@ -138,6 +138,15 @@
         whole_ref[:, :span] = other_ref[...]
         whole_ref[:, span:] = own_ref[...]
 
+    for block in range(0, blocks, 2):
+        low, high = max(block - 1, 0), min(block + 3, blocks)
+        part = band_ref[(low - block + 1) * LANES : (high - block + 1) * LANES, :]
+        got = jnp.dot(
+            whole_ref[:, low * LANES : high * LANES], part, preferred_element_type=jnp.float32
+        )
+        level_ref[block * rows : (block + 1) * rows, :] = got[:, :LANES]
+        level_ref[(block + 1) * rows : (block + 2) * rows, :] = got[:, LANES:]
+
     carried = {}
 
     def moved(tiles, at_row):
@@ -153,13 +162,6 @@
 
     ends = []
     for block in range(0, blocks, 2):
-        low, high = max(block - 1, 0), min(block + 3, blocks)
-        part = band_ref[(low - block + 1) * LANES : (high - block + 1) * LANES, :]
-        got = jnp.dot(
-            whole_ref[:, low * LANES : high * LANES], part, preferred_element_type=jnp.float32
-        )
-        level_ref[block * rows : (block + 1) * rows, :] = got[:, :LANES]
-        level_ref[(block + 1) * rows : (block + 2) * rows, :] = got[:, LANES:]
         bands = []
         for e in range(trials):
             scale = gain_ref[e * SUBLANES : (e + 1) * SUBLANES, :]

time: 17.3 us -> 17.3 us (level)
  no operation moved by 1% of the time
where the time goes in v4:
time: 17.3 us; the launch traced here: 17.1 us
  starting transfers between devices  8.17 us (47%)
  waiting for transfers between devices  5.84 us (34%)
  Pallas kernels  3.05 us (18%)
    ppermute x3, starting transfers between devices, shards(): lax.ppermute(plane, ('sub', 'tm'), [(i, i ^ mask) for i in range(subs * s...  7.3 us
    ppermute x3, waiting for transfers between devices, shards(): lax.ppermute(plane, ('sub', 'tm'), [(i, i ^ mask) for i in range(subs * s...  4.8 us
    pallas_call x1, Pallas kernels, shards(): pl.pallas_call(functools.partial(plane_kernel, trials), out_shape=tiled(s...  1.19 us
    pallas_call x1, Pallas kernels, shards(): pl.pallas_call(table_kernel, out_shape=(jax.ShapeDtypeStruct(filterbank.s...  0.99 us
    ppermute x1, waiting for transfers between devices, shards(): lax.ppermute(send, 'tm', swap)  0.84 us
    pallas_call x1, Pallas kernels, shards(): call(functools.partial(last_kernel, cross_levels), out_shape=jax.ShapeDty...  0.63 us
    ppermute x1, starting transfers between devices, shards(): other = lax.ppermute(filterbank, 'tm', swap)  0.45 us
    ppermute x1, starting transfers between devices, shards(): lax.ppermute(send, 'tm', swap)  0.42 us
  transfers between devices with their start and end apart: 5, of which 5 were waited for; matrix products, arithmetic and copies ran while one was open for 0% of the time, Pallas kernels for 6%

profile of v4, /device:TPU:0, one launch (start us, length us, event | category | flops | bytes accessed | tf_op | source)
XLA Modules:
  0.0 17.1 jit_solution(15764267224793300524)
XLA Ops:
  0.0 0.5 %collective-permute-start = (bf16[128,512]{1,0:T(8,128)(2,1)}, bf16[128,512]{1,0:T(8,128)(2,1)S(1)}, u32[]{:S(2)}, u32[]{:S(2)}) collective-permute-start(bf16[128,512]{1,0:T(8,128)(2,1)} %refs_0_.1), channel_id=1, source_target_pairs={{0,1},{1,0},{2,3},{3,2},{4,5},{5,4},{6,7},{7,6},{8,9},{9,8},{10,11... | collective-permute-start | bytes 393224 | tf_op jit(solution)/shard_map/ppermute | solution.py:247
  0.5 1.0 %shard_map.46 = (bf16[128,512]{1,0:T(8,128)(2,1)S(1)}, s32[384,128]{1,0:T(8,128)S(1)}, f32[128,128]{1,0:T(8,128)S(1)}, s32[24,128]{1,0:T(8,128)S(1)}, bf16[512,256]{1,0:T(8,128)(2,1)S(1)}) custom-call(bf16[128,512]{1,0:T(8,128)(2,1)} %refs_0_.1, f32[1,128]{1,0:T(1,128)} %bitcast.1, s32[7,128]{1,0:T(8,128)} %refs_2_.1, s32[3,16]{1,0:T(4,128)} %refs_3_.1), custom_call_target="tpu_custom_call" | custom-call | tf_op jit(solution)/shard_map/pallas_call | solution.py:249
  1.4 0.2 %collective-permute-done.other_ref = bf16[128,512]{1,0:T(8,128)(2,1)S(1)} collective-permute-done((bf16[128,512]{1,0:T(8,128)(2,1)}, bf16[128,512]{1,0:T(8,128)(2,1)S(1)}, u32[]{:S(2)}, u32[]{:S(2)}) %collective-permute-start) | collective-permute-done | bytes 131104 | tf_op jit(solution)/shard_map/ppermute | solution.py:247
  1.7 1.2 %shard_map.47.own_ref = f32[64,128]{1,0:T(8,128)S(1)} custom-call(bf16[128,512]{1,0:T(8,128)(2,1)S(1)} %get-tuple-element.12.own_ref, bf16[128,512]{1,0:T(8,128)(2,1)S(1)} %collective-permute-done.other_ref, s32[384,128]{1,0:T(8,128)S(1)} %get-tuple-element.13.shifts_ref, f32[128,128]{1,0:T(8,128)S(1)} %get-tuple-element.14.gain_ref, ...), custom_call_target="tpu_custom_call" | custom-call | tf_op jit(solution)/shard_map/pallas_call | solution.py:264
  2.8 2.7 %collective-permute-start.1 = (f32[64,128]{1,0:T(8,128)S(1)}, f32[64,128]{1,0:T(8,128)S(1)}, u32[]{:S(2)}, u32[]{:S(2)}) collective-permute-start(f32[64,128]{1,0:T(8,128)S(1)} %shard_map.47.own_ref), channel_id=1, source_target_pairs={{0,3},{1,2},{2,1},{3,0},{4,7},{5,6},{6,5},{7,4},{8,11},{9,10},{10,... | collective-permute-start | bytes 98312 | tf_op jit(solution)/shard_map/ppermute | solution.py:278
  5.5 1.6 %collective-permute-done.1.there_ref = f32[64,128]{1,0:T(8,128)S(1)} collective-permute-done((f32[64,128]{1,0:T(8,128)S(1)}, f32[64,128]{1,0:T(8,128)S(1)}, u32[]{:S(2)}, u32[]{:S(2)}) %collective-permute-start.1) | collective-permute-done | bytes 32800 | tf_op jit(solution)/shard_map/ppermute | solution.py:278
  7.1 0.1 shard_map.48.own_ref
  7.2 1.9 %collective-permute-start.2 = (f32[64,128]{1,0:T(8,128)S(1)}, f32[64,128]{1,0:T(8,128)S(1)}, u32[]{:S(2)}, u32[]{:S(2)}) collective-permute-start(f32[64,128]{1,0:T(8,128)S(1)} %shard_map.48.own_ref), channel_id=1, source_target_pairs={{0,5},{1,4},{2,7},{3,6},{4,1},{5,0},{6,3},{7,2},{8,13},{9,12},{10,... | collective-permute-start | bytes 98312 | tf_op jit(solution)/shard_map/ppermute | solution.py:278
  9.1 1.6 %collective-permute-done.2.there_ref = f32[64,128]{1,0:T(8,128)S(1)} collective-permute-done((f32[64,128]{1,0:T(8,128)S(1)}, f32[64,128]{1,0:T(8,128)S(1)}, u32[]{:S(2)}, u32[]{:S(2)}) %collective-permute-start.2) | collective-permute-done | bytes 32800 | tf_op jit(solution)/shard_map/ppermute | solution.py:278
  10.7 0.1 shard_map.49.own_ref
  10.7 2.8 %collective-permute-start.3 = (f32[64,128]{1,0:T(8,128)S(1)}, f32[64,128]{1,0:T(8,128)S(1)}, u32[]{:S(2)}, u32[]{:S(2)}) collective-permute-start(f32[64,128]{1,0:T(8,128)S(1)} %shard_map.49.own_ref), channel_id=1, source_target_pairs={{0,9},{1,8},{2,11},{3,10},{4,13},{5,12},{6,15},{7,14},{8,1},{9,0},... | collective-permute-start | bytes 98312 | tf_op jit(solution)/shard_map/ppermute | solution.py:278
  13.5 1.6 %collective-permute-done.3.there_ref = f32[64,128]{1,0:T(8,128)S(1)} collective-permute-done((f32[64,128]{1,0:T(8,128)S(1)}, f32[64,128]{1,0:T(8,128)S(1)}, u32[]{:S(2)}, u32[]{:S(2)}) %collective-permute-start.3) | collective-permute-done | bytes 32800 | tf_op jit(solution)/shard_map/ppermute | solution.py:278
  15.1 0.1 shard_map.50
  15.2 0.4 %collective-permute-start.4 = (f32[32,128]{1,0:T(8,128)S(1)}, f32[32,128]{1,0:T(8,128)S(1)}, u32[]{:S(2)}, u32[]{:S(2)}) collective-permute-start(f32[32,128]{1,0:T(8,128)S(1)} %get-tuple-element.18), channel_id=1, source_target_pairs={{0,1},{1,0},{2,3},{3,2},{4,5},{5,4},{6,7},{7,6},{8,9},{9,8},{10,11... | collective-permute-start | bytes 49160 | tf_op jit(solution)/shard_map/ppermute | solution.py:292
  15.6 0.8 %collective-permute-done.4.there_ref = f32[32,128]{1,0:T(8,128)S(1)} collective-permute-done((f32[32,128]{1,0:T(8,128)S(1)}, f32[32,128]{1,0:T(8,128)S(1)}, u32[]{:S(2)}, u32[]{:S(2)}) %collective-permute-start.4) | collective-permute-done | bytes 16416 | tf_op jit(solution)/shard_map/ppermute | solution.py:292
  16.5 0.6 %shard_map.51 = f32[16,512]{1,0:T(8,128)} custom-call(f32[32,128]{1,0:T(8,128)S(1)} %get-tuple-element.17.keep_ref, f32[32,128]{1,0:T(8,128)S(1)} %collective-permute-done.4.there_ref), custom_call_target="tpu_custom_call" | custom-call | tf_op jit(solution)/shard_map/pallas_call | solution.py:287
Async XLA Ops:
  0.0 1.6 %collective-permute-start = (bf16[128,512]{1,0:T(8,128)(2,1)}, bf16[128,512]{1,0:T(8,128)(2,1)S(1)}, u32[]{:S(2)}, u32[]{:S(2)}) collective-permute-start(bf16[128,512]{1,0:T(8,128)(2,1)} %refs_0_.1), channel_id=1, source_target_pairs={{0,1},{1,0},{2,3},{3,2},{4,5},{5,4},{6,7},{7,6},{8,9},{9,8},{10,11... | collective-permute-start | bytes 393224 | tf_op jit(solution)/shard_map/ppermute | solution.py:247
  2.8 4.3 %collective-permute-start.1 = (f32[64,128]{1,0:T(8,128)S(1)}, f32[64,128]{1,0:T(8,128)S(1)}, u32[]{:S(2)}, u32[]{:S(2)}) collective-permute-start(f32[64,128]{1,0:T(8,128)S(1)} %shard_map.47.own_ref), channel_id=1, source_target_pairs={{0,3},{1,2},{2,1},{3,0},{4,7},{5,6},{6,5},{7,4},{8,11},{9,10},{10,... | collective-permute-start | bytes 98312 | tf_op jit(solution)/shard_map/ppermute | solution.py:278
  7.2 3.5 %collective-permute-start.2 = (f32[64,128]{1,0:T(8,128)S(1)}, f32[64,128]{1,0:T(8,128)S(1)}, u32[]{:S(2)}, u32[]{:S(2)}) collective-permute-start(f32[64,128]{1,0:T(8,128)S(1)} %shard_map.48.own_ref), channel_id=1, source_target_pairs={{0,5},{1,4},{2,7},{3,6},{4,1},{5,0},{6,3},{7,2},{8,13},{9,12},{10,... | collective-permute-start | bytes 98312 | tf_op jit(solution)/shard_map/ppermute | solution.py:278
  10.7 4.4 %collective-permute-start.3 = (f32[64,128]{1,0:T(8,128)S(1)}, f32[64,128]{1,0:T(8,128)S(1)}, u32[]{:S(2)}, u32[]{:S(2)}) collective-permute-start(f32[64,128]{1,0:T(8,128)S(1)} %shard_map.49.own_ref), channel_id=1, source_target_pairs={{0,9},{1,8},{2,11},{3,10},{4,13},{5,12},{6,15},{7,14},{8,1},{9,0},... | collective-permute-start | bytes 98312 | tf_op jit(solution)/shard_map/ppermute | solution.py:278
  15.2 1.3 %collective-permute-start.4 = (f32[32,128]{1,0:T(8,128)S(1)}, f32[32,128]{1,0:T(8,128)S(1)}, u32[]{:S(2)}, u32[]{:S(2)}) collective-permute-start(f32[32,128]{1,0:T(8,128)S(1)} %get-tuple-element.18), channel_id=1, source_target_pairs={{0,1},{1,0},{2,3},{3,2},{4,5},{5,4},{6,7},{7,6},{8,9},{9,8},{10,11... | collective-permute-start | bytes 49160 | tf_op jit(solution)/shard_map/ppermute | solution.py:292

commit v5 on v0

--- a/solution.py
+++ b/solution.py
@@ -121,28 +121,22 @@
     copies[-1].wait()
 
 
-def plane_kernel(trials, own_ref, other_ref, shifts_ref, gain_ref, band_ref, out_ref, whole_ref, level_ref):
+def plane_kernel(trials, own_ref, other_ref, shifts_ref, gain_ref, band_ref, out_ref, level_ref):
     rows, span = own_ref.shape
     grow = trials.bit_length() - 1
-    columns = whole_ref.shape[1]
-    blocks = columns // LANES
     first_span = lax.axis_index("tm") == 0
-
-    @pl.when(first_span)
-    def _():
-        whole_ref[:, :span] = own_ref[...]
-        whole_ref[:, span:] = other_ref[...]
-
-    @pl.when(jnp.logical_not(first_span))
-    def _():
-        whole_ref[:, :span] = other_ref[...]
-        whole_ref[:, span:] = own_ref[...]
+    own, other = (
+        [ref[:, start : start + LANES] for start in range(0, span, LANES)] for ref in (own_ref, other_ref)
+    )
+    whole = [jnp.where(first_span, a, b) for a, b in zip(own, other)]
+    whole += [jnp.where(first_span, b, a) for a, b in zip(own, other)]
+    blocks = len(whole)
 
     for block in range(0, blocks, 2):
         low, high = max(block - 1, 0), min(block + 3, blocks)
         part = band_ref[(low - block + 1) * LANES : (high - block + 1) * LANES, :]
         got = jnp.dot(
-            whole_ref[:, low * LANES : high * LANES], part, preferred_element_type=jnp.float32
+            jnp.concatenate(whole[low:high], axis=1), part, preferred_element_type=jnp.float32
         )
         level_ref[block * rows : (block + 1) * rows, :] = got[:, :LANES]
         level_ref[(block + 1) * rows : (block + 2) * rows, :] = got[:, LANES:]
@@ -255,10 +249,7 @@
         out_shape=tiled(spans * past),
         in_specs=[vmem] * 5,
         out_specs=vmem,
-        scratch_shapes=[
-            pltpu.VMEM((rows, spans * span), filterbank.dtype),
-            pltpu.VMEM((rows * spans * past, LANES), jnp.float32),
-        ],
+        scratch_shapes=[pltpu.VMEM((rows * spans * past, LANES), jnp.float32)],
         compiler_params=room(6),
     )(own, other, shifts, gain, band)
     for level in range(cross_levels):

time: 17.1 us -> 17.1 us (level)
  no operation moved by 1% of the time
where the time goes in v5:
time: 17.1 us; the launch traced here: 16.8 us
  starting transfers between devices  8.17 us (48%)
  waiting for transfers between devices  5.84 us (34%)
  Pallas kernels  2.81 us (16%)
    ppermute x3, starting transfers between devices, shards(): lax.ppermute(plane, ('sub', 'tm'), [(i, i ^ mask) for i in range(subs * s...  7.3 us
    ppermute x3, waiting for transfers between devices, shards(): lax.ppermute(plane, ('sub', 'tm'), [(i, i ^ mask) for i in range(subs * s...  4.8 us
    pallas_call x1, Pallas kernels, shards(): pl.pallas_call(table_kernel, out_shape=(jax.ShapeDtypeStruct(filterbank.s...  0.99 us
    pallas_call x1, Pallas kernels, shards(): pl.pallas_call(functools.partial(plane_kernel, trials), out_shape=tiled(s...  0.95 us
    ppermute x1, waiting for transfers between devices, shards(): lax.ppermute(send, 'tm', swap)  0.84 us
    pallas_call x1, Pallas kernels, shards(): call(functools.partial(last_kernel, cross_levels), out_shape=jax.ShapeDty...  0.63 us
    ppermute x1, starting transfers between devices, shards(): other = lax.ppermute(filterbank, 'tm', swap)  0.45 us
    ppermute x1, starting transfers between devices, shards(): lax.ppermute(send, 'tm', swap)  0.42 us
  transfers between devices with their start and end apart: 5, of which 5 were waited for; matrix products, arithmetic and copies ran while one was open for 0% of the time, Pallas kernels for 6%

profile of v5, /device:TPU:0, one launch (start us, length us, event | category | flops | bytes accessed | tf_op | source)
XLA Modules:
  0.0 16.8 jit_solution(13162316911960080940)
XLA Ops:
  0.0 0.5 %collective-permute-start = (bf16[128,512]{1,0:T(8,128)(2,1)}, bf16[128,512]{1,0:T(8,128)(2,1)S(1)}, u32[]{:S(2)}, u32[]{:S(2)}) collective-permute-start(bf16[128,512]{1,0:T(8,128)(2,1)} %refs_0_.1), channel_id=1, source_target_pairs={{0,1},{1,0},{2,3},{3,2},{4,5},{5,4},{6,7},{7,6},{8,9},{9,8},{10,11... | collective-permute-start | bytes 393224 | tf_op jit(solution)/shard_map/ppermute | solution.py:230
  0.5 1.0 %shard_map.46 = (bf16[128,512]{1,0:T(8,128)(2,1)S(1)}, s32[384,128]{1,0:T(8,128)S(1)}, f32[128,128]{1,0:T(8,128)S(1)}, s32[24,128]{1,0:T(8,128)S(1)}, bf16[512,256]{1,0:T(8,128)(2,1)S(1)}) custom-call(bf16[128,512]{1,0:T(8,128)(2,1)} %refs_0_.1, f32[1,128]{1,0:T(1,128)} %bitcast.1, s32[7,128]{1,0:T(8,128)} %refs_2_.1, s32[3,16]{1,0:T(4,128)} %refs_3_.1), custom_call_target="tpu_custom_call" | custom-call | tf_op jit(solution)/shard_map/pallas_call | solution.py:232
  1.4 0.2 %collective-permute-done.other_ref = bf16[128,512]{1,0:T(8,128)(2,1)S(1)} collective-permute-done((bf16[128,512]{1,0:T(8,128)(2,1)}, bf16[128,512]{1,0:T(8,128)(2,1)S(1)}, u32[]{:S(2)}, u32[]{:S(2)}) %collective-permute-start) | collective-permute-done | bytes 131104 | tf_op jit(solution)/shard_map/ppermute | solution.py:230
  1.7 1.0 %shard_map.47.own_ref = f32[64,128]{1,0:T(8,128)S(1)} custom-call(bf16[128,512]{1,0:T(8,128)(2,1)S(1)} %get-tuple-element.12.own_ref, bf16[128,512]{1,0:T(8,128)(2,1)S(1)} %collective-permute-done.other_ref, s32[384,128]{1,0:T(8,128)S(1)} %get-tuple-element.13.shifts_ref, f32[128,128]{1,0:T(8,128)S(1)} %get-tuple-element.14.gain_ref, ...), custom_call_target="tpu_custom_call" | custom-call | tf_op jit(solution)/shard_map/pallas_call | solution.py:247
  2.6 2.7 %collective-permute-start.1 = (f32[64,128]{1,0:T(8,128)S(1)}, f32[64,128]{1,0:T(8,128)S(1)}, u32[]{:S(2)}, u32[]{:S(2)}) collective-permute-start(f32[64,128]{1,0:T(8,128)S(1)} %shard_map.47.own_ref), channel_id=1, source_target_pairs={{0,3},{1,2},{2,1},{3,0},{4,7},{5,6},{6,5},{7,4},{8,11},{9,10},{10,... | collective-permute-start | bytes 98312 | tf_op jit(solution)/shard_map/ppermute | solution.py:258
  5.3 1.6 %collective-permute-done.1.there_ref = f32[64,128]{1,0:T(8,128)S(1)} collective-permute-done((f32[64,128]{1,0:T(8,128)S(1)}, f32[64,128]{1,0:T(8,128)S(1)}, u32[]{:S(2)}, u32[]{:S(2)}) %collective-permute-start.1) | collective-permute-done | bytes 32800 | tf_op jit(solution)/shard_map/ppermute | solution.py:258
  6.9 0.1 shard_map.48.own_ref
  7.0 1.9 %collective-permute-start.2 = (f32[64,128]{1,0:T(8,128)S(1)}, f32[64,128]{1,0:T(8,128)S(1)}, u32[]{:S(2)}, u32[]{:S(2)}) collective-permute-start(f32[64,128]{1,0:T(8,128)S(1)} %shard_map.48.own_ref), channel_id=1, source_target_pairs={{0,5},{1,4},{2,7},{3,6},{4,1},{5,0},{6,3},{7,2},{8,13},{9,12},{10,... | collective-permute-start | bytes 98312 | tf_op jit(solution)/shard_map/ppermute | solution.py:258
  8.8 1.6 %collective-permute-done.2.there_ref = f32[64,128]{1,0:T(8,128)S(1)} collective-permute-done((f32[64,128]{1,0:T(8,128)S(1)}, f32[64,128]{1,0:T(8,128)S(1)}, u32[]{:S(2)}, u32[]{:S(2)}) %collective-permute-start.2) | collective-permute-done | bytes 32800 | tf_op jit(solution)/shard_map/ppermute | solution.py:258
  10.4 0.1 shard_map.49.own_ref
  10.5 2.8 %collective-permute-start.3 = (f32[64,128]{1,0:T(8,128)S(1)}, f32[64,128]{1,0:T(8,128)S(1)}, u32[]{:S(2)}, u32[]{:S(2)}) collective-permute-start(f32[64,128]{1,0:T(8,128)S(1)} %shard_map.49.own_ref), channel_id=1, source_target_pairs={{0,9},{1,8},{2,11},{3,10},{4,13},{5,12},{6,15},{7,14},{8,1},{9,0},... | collective-permute-start | bytes 98312 | tf_op jit(solution)/shard_map/ppermute | solution.py:258
  13.3 1.6 %collective-permute-done.3.there_ref = f32[64,128]{1,0:T(8,128)S(1)} collective-permute-done((f32[64,128]{1,0:T(8,128)S(1)}, f32[64,128]{1,0:T(8,128)S(1)}, u32[]{:S(2)}, u32[]{:S(2)}) %collective-permute-start.3) | collective-permute-done | bytes 32800 | tf_op jit(solution)/shard_map/ppermute | solution.py:258
  14.9 0.1 shard_map.50
  15.0 0.4 %collective-permute-start.4 = (f32[32,128]{1,0:T(8,128)S(1)}, f32[32,128]{1,0:T(8,128)S(1)}, u32[]{:S(2)}, u32[]{:S(2)}) collective-permute-start(f32[32,128]{1,0:T(8,128)S(1)} %get-tuple-element.18), channel_id=1, source_target_pairs={{0,1},{1,0},{2,3},{3,2},{4,5},{5,4},{6,7},{7,6},{8,9},{9,8},{10,11... | collective-permute-start | bytes 49160 | tf_op jit(solution)/shard_map/ppermute | solution.py:272
  15.4 0.8 %collective-permute-done.4.there_ref = f32[32,128]{1,0:T(8,128)S(1)} collective-permute-done((f32[32,128]{1,0:T(8,128)S(1)}, f32[32,128]{1,0:T(8,128)S(1)}, u32[]{:S(2)}, u32[]{:S(2)}) %collective-permute-start.4) | collective-permute-done | bytes 16416 | tf_op jit(solution)/shard_map/ppermute | solution.py:272
  16.2 0.6 %shard_map.51 = f32[16,512]{1,0:T(8,128)} custom-call(f32[32,128]{1,0:T(8,128)S(1)} %get-tuple-element.17.keep_ref, f32[32,128]{1,0:T(8,128)S(1)} %collective-permute-done.4.there_ref), custom_call_target="tpu_custom_call" | custom-call | tf_op jit(solution)/shard_map/pallas_call | solution.py:267
Async XLA Ops:
  0.0 1.6 %collective-permute-start = (bf16[128,512]{1,0:T(8,128)(2,1)}, bf16[128,512]{1,0:T(8,128)(2,1)S(1)}, u32[]{:S(2)}, u32[]{:S(2)}) collective-permute-start(bf16[128,512]{1,0:T(8,128)(2,1)} %refs_0_.1), channel_id=1, source_target_pairs={{0,1},{1,0},{2,3},{3,2},{4,5},{5,4},{6,7},{7,6},{8,9},{9,8},{10,11... | collective-permute-start | bytes 393224 | tf_op jit(solution)/shard_map/ppermute | solution.py:230
  2.6 4.3 %collective-permute-start.1 = (f32[64,128]{1,0:T(8,128)S(1)}, f32[64,128]{1,0:T(8,128)S(1)}, u32[]{:S(2)}, u32[]{:S(2)}) collective-permute-start(f32[64,128]{1,0:T(8,128)S(1)} %shard_map.47.own_ref), channel_id=1, source_target_pairs={{0,3},{1,2},{2,1},{3,0},{4,7},{5,6},{6,5},{7,4},{8,11},{9,10},{10,... | collective-permute-start | bytes 98312 | tf_op jit(solution)/shard_map/ppermute | solution.py:258
  7.0 3.5 %collective-permute-start.2 = (f32[64,128]{1,0:T(8,128)S(1)}, f32[64,128]{1,0:T(8,128)S(1)}, u32[]{:S(2)}, u32[]{:S(2)}) collective-permute-start(f32[64,128]{1,0:T(8,128)S(1)} %shard_map.48.own_ref), channel_id=1, source_target_pairs={{0,5},{1,4},{2,7},{3,6},{4,1},{5,0},{6,3},{7,2},{8,13},{9,12},{10,... | collective-permute-start | bytes 98312 | tf_op jit(solution)/shard_map/ppermute | solution.py:258
  10.5 4.4 %collective-permute-start.3 = (f32[64,128]{1,0:T(8,128)S(1)}, f32[64,128]{1,0:T(8,128)S(1)}, u32[]{:S(2)}, u32[]{:S(2)}) collective-permute-start(f32[64,128]{1,0:T(8,128)S(1)} %shard_map.49.own_ref), channel_id=1, source_target_pairs={{0,9},{1,8},{2,11},{3,10},{4,13},{5,12},{6,15},{7,14},{8,1},{9,0},... | collective-permute-start | bytes 98312 | tf_op jit(solution)/shard_map/ppermute | solution.py:258
  15.0 1.3 %collective-permute-start.4 = (f32[32,128]{1,0:T(8,128)S(1)}, f32[32,128]{1,0:T(8,128)S(1)}, u32[]{:S(2)}, u32[]{:S(2)}) collective-permute-start(f32[32,128]{1,0:T(8,128)S(1)} %get-tuple-element.18), channel_id=1, source_target_pairs={{0,1},{1,0},{2,3},{3,2},{4,5},{5,4},{6,7},{7,6},{8,9},{9,8},{10,11... | collective-permute-start | bytes 49160 | tf_op jit(solution)/shard_map/ppermute | solution.py:272

commit v6 on v2

--- a/solution.py
+++ b/solution.py
@@ -143,15 +143,22 @@
     per_span = span // LANES
     blocks = 2 * per_span
     first_span = lax.axis_index("tm") == 0
-    window_sums(other_ref, band_ref, other_level_ref)
-
-    own_early, own_late = own_ref[:, span - LANES :], own_ref[:, :LANES]
-    other_early, other_late = other_ref[:, span - LANES :], other_ref[:, :LANES]
-    early = jnp.where(first_span, own_early, other_early)
-    late = jnp.where(first_span, other_late, own_late)
+    own_first, own_last = own_ref[:, :LANES], own_ref[:, span - LANES :]
+    none = jnp.zeros((rows, LANES), own_ref.dtype)
+    other = [other_ref[:, start : start + LANES] for start in range(0, span, LANES)]
+    about = [jnp.where(first_span, own_last, none), *other, jnp.where(first_span, none, own_first)]
+    for block in range(0, per_span, 2):
+        window = jnp.concatenate(about[block : block + 4], axis=1)
+        got = jnp.dot(window, band_ref[...], preferred_element_type=jnp.float32)
+        other_level_ref[block * rows : (block + 1) * rows, :] = got[:, :LANES]
+        other_level_ref[(block + 1) * rows : (block + 2) * rows, :] = got[:, LANES:]
+
     after, before = band_ref[3 * LANES :, LANES:], band_ref[:LANES, :LANES]
-    seam_ref[:rows, :] = jnp.dot(late, after, preferred_element_type=jnp.float32)
-    seam_ref[rows:, :] = jnp.dot(early, before, preferred_element_type=jnp.float32)
+    seam_ref[...] = jnp.dot(
+        jnp.where(first_span, other[0], other[-1]),
+        jnp.where(first_span, after, before),
+        preferred_element_type=jnp.float32,
+    )
 
     bands = []
     for e in range(trials):
@@ -161,8 +168,9 @@
         other = [rows_of(other_level_ref, block) for block in range(per_span)]
         tiles = [jnp.where(first_span, a, b) for a, b in zip(own, other)]
         tiles += [jnp.where(first_span, b, a) for a, b in zip(own, other)]
-        tiles[per_span - 1] += rows_of(seam_ref, 0)
-        tiles[per_span] += rows_of(seam_ref, 1)
+        seam = rows_of(seam_ref, 0)
+        tiles[per_span - 1] += jnp.where(first_span, seam, 0.0)
+        tiles[per_span] += jnp.where(first_span, 0.0, seam)
         bands.append([tile * scale for tile in tiles])
     plane = [bands]
 
@@ -269,7 +277,7 @@
         out_specs=vmem,
         scratch_shapes=[
             pltpu.VMEM((rows * past, LANES), jnp.float32),
-            pltpu.VMEM((rows * 2, LANES), jnp.float32),
+            pltpu.VMEM((rows, LANES), jnp.float32),
         ],
         compiler_params=room(6),
     )(own, other, own_level, shifts, gain, band)

time: 17 us -> 17 us (level)
  no operation moved by 1% of the time
where the time goes in v6:
time: 17 us; the launch traced here: 16.9 us
  starting transfers between devices  8.04 us (47%)
  waiting for transfers between devices  5.72 us (34%)
  Pallas kernels  3.08 us (18%)
    ppermute x3, starting transfers between devices, shards(): lax.ppermute(plane, ('sub', 'tm'), [(i, i ^ mask) for i in range(subs * s...  7.26 us
    ppermute x3, waiting for transfers between devices, shards(): lax.ppermute(plane, ('sub', 'tm'), [(i, i ^ mask) for i in range(subs * s...  4.8 us
    pallas_call x1, Pallas kernels, shards(): pl.pallas_call(table_kernel, out_shape=(jax.ShapeDtypeStruct(filterbank.s...  1.27 us
    pallas_call x1, Pallas kernels, shards(): pl.pallas_call(functools.partial(plane_kernel, trials), out_shape=tiled(s...  0.93 us
    ppermute x1, waiting for transfers between devices, shards(): lax.ppermute(send, 'tm', swap)  0.92 us
    pallas_call x1, Pallas kernels, shards(): call(functools.partial(last_kernel, cross_levels), out_shape=jax.ShapeDty...  0.63 us
    ppermute x1, starting transfers between devices, shards(): other = lax.ppermute(filterbank, 'tm', swap)  0.45 us
  transfers between devices with their start and end apart: 5, of which 4 were waited for; matrix products, arithmetic and copies ran while one was open for 0% of the time, Pallas kernels for 8%

profile of v6, /device:TPU:0, one launch (start us, length us, event | category | flops | bytes accessed | tf_op | source)
XLA Modules:
  0.0 16.9 jit_solution(13135143928551848670)
XLA Ops:
  0.0 0.5 %collective-permute-start = (bf16[128,512]{1,0:T(8,128)(2,1)}, bf16[128,512]{1,0:T(8,128)(2,1)S(1)}, u32[]{:S(2)}, u32[]{:S(2)}) collective-permute-start(bf16[128,512]{1,0:T(8,128)(2,1)} %refs_0_.1), channel_id=1, source_target_pairs={{0,1},{1,0},{2,3},{3,2},{4,5},{5,4},{6,7},{7,6},{8,9},{9,8},{10,11... | collective-permute-start | bytes 393224 | tf_op jit(solution)/shard_map/ppermute | solution.py:255
  0.5 1.3 %shard_map.46 = (bf16[128,512]{1,0:T(8,128)(2,1)S(1)}, f32[512,128]{1,0:T(8,128)S(1)}, s32[384,128]{1,0:T(8,128)S(1)}, f32[128,128]{1,0:T(8,128)S(1)}, s32[24,12...) custom-call(bf16[128,512]{1,0:T(8,128)(2,1)} %refs_0_.1, f32[1,128]{1,0:T(1,128)} %bitcast.1, s32[7,128]{1,0:T(8,128)} %refs_2_.1, ...), custom_call_target="tpu_custom_call" | custom-call | tf_op jit(solution)/shard_map/pallas_call | solution.py:257
  1.7 0.0 collective-permute-done.refs_1_
  1.7 0.9 %shard_map.47.own_ref = f32[64,128]{1,0:T(8,128)S(1)} custom-call(bf16[128,512]{1,0:T(8,128)(2,1)S(1)} %get-tuple-element.13.refs_0_, bf16[128,512]{1,0:T(8,128)(2,1)S(1)} %collective-permute-done.refs_1_, f32[512,128]{1,0:T(8,128)S(1)} %get-tuple-element.14.refs_2_, s32[384,128]{1,0:T(8,128)S(1)} %get-tuple-element.15.refs_3_, ...), custom_call_target="tpu_custom_call" | custom-call | tf_op jit(solution)/shard_map/pallas_call | solution.py:273
  2.7 2.7 %collective-permute-start.1 = (f32[64,128]{1,0:T(8,128)S(1)}, f32[64,128]{1,0:T(8,128)S(1)}, u32[]{:S(2)}, u32[]{:S(2)}) collective-permute-start(f32[64,128]{1,0:T(8,128)S(1)} %shard_map.47.own_ref), channel_id=1, source_target_pairs={{0,3},{1,2},{2,1},{3,0},{4,7},{5,6},{6,5},{7,4},{8,11},{9,10},{10,... | collective-permute-start | bytes 98312 | tf_op jit(solution)/shard_map/ppermute | solution.py:287
  5.3 1.6 %collective-permute-done.1.there_ref = f32[64,128]{1,0:T(8,128)S(1)} collective-permute-done((f32[64,128]{1,0:T(8,128)S(1)}, f32[64,128]{1,0:T(8,128)S(1)}, u32[]{:S(2)}, u32[]{:S(2)}) %collective-permute-start.1) | collective-permute-done | bytes 32800 | tf_op jit(solution)/shard_map/ppermute | solution.py:287
  6.9 0.1 shard_map.48.own_ref
  7.0 1.8 %collective-permute-start.2 = (f32[64,128]{1,0:T(8,128)S(1)}, f32[64,128]{1,0:T(8,128)S(1)}, u32[]{:S(2)}, u32[]{:S(2)}) collective-permute-start(f32[64,128]{1,0:T(8,128)S(1)} %shard_map.48.own_ref), channel_id=1, source_target_pairs={{0,5},{1,4},{2,7},{3,6},{4,1},{5,0},{6,3},{7,2},{8,13},{9,12},{10,... | collective-permute-start | bytes 98312 | tf_op jit(solution)/shard_map/ppermute | solution.py:287
  8.9 1.6 %collective-permute-done.2.there_ref = f32[64,128]{1,0:T(8,128)S(1)} collective-permute-done((f32[64,128]{1,0:T(8,128)S(1)}, f32[64,128]{1,0:T(8,128)S(1)}, u32[]{:S(2)}, u32[]{:S(2)}) %collective-permute-start.2) | collective-permute-done | bytes 32800 | tf_op jit(solution)/shard_map/ppermute | solution.py:287
  10.5 0.1 shard_map.49.own_ref
  10.5 2.8 %collective-permute-start.3 = (f32[64,128]{1,0:T(8,128)S(1)}, f32[64,128]{1,0:T(8,128)S(1)}, u32[]{:S(2)}, u32[]{:S(2)}) collective-permute-start(f32[64,128]{1,0:T(8,128)S(1)} %shard_map.49.own_ref), channel_id=1, source_target_pairs={{0,9},{1,8},{2,11},{3,10},{4,13},{5,12},{6,15},{7,14},{8,1},{9,0},... | collective-permute-start | bytes 98312 | tf_op jit(solution)/shard_map/ppermute | solution.py:287
  13.3 1.6 %collective-permute-done.3.there_ref = f32[64,128]{1,0:T(8,128)S(1)} collective-permute-done((f32[64,128]{1,0:T(8,128)S(1)}, f32[64,128]{1,0:T(8,128)S(1)}, u32[]{:S(2)}, u32[]{:S(2)}) %collective-permute-start.3) | collective-permute-done | bytes 32800 | tf_op jit(solution)/shard_map/ppermute | solution.py:287
  14.9 0.1 shard_map.50
  15.0 0.3 %collective-permute-start.4 = (f32[32,128]{1,0:T(8,128)S(1)}, f32[32,128]{1,0:T(8,128)S(1)}, u32[]{:S(2)}, u32[]{:S(2)}) collective-permute-start(f32[32,128]{1,0:T(8,128)S(1)} %get-tuple-element.20), channel_id=1, source_target_pairs={{0,1},{1,0},{2,3},{3,2},{4,5},{5,4},{6,7},{7,6},{8,9},{9,8},{10,11... | collective-permute-start | bytes 49160 | tf_op jit(solution)/shard_map/ppermute | solution.py:301
  15.3 0.9 %collective-permute-done.4.there_ref = f32[32,128]{1,0:T(8,128)S(1)} collective-permute-done((f32[32,128]{1,0:T(8,128)S(1)}, f32[32,128]{1,0:T(8,128)S(1)}, u32[]{:S(2)}, u32[]{:S(2)}) %collective-permute-start.4) | collective-permute-done | bytes 16416 | tf_op jit(solution)/shard_map/ppermute | solution.py:301
  16.2 0.6 %shard_map.51 = f32[16,512]{1,0:T(8,128)} custom-call(f32[32,128]{1,0:T(8,128)S(1)} %get-tuple-element.19.keep_ref, f32[32,128]{1,0:T(8,128)S(1)} %collective-permute-done.4.there_ref), custom_call_target="tpu_custom_call" | custom-call | tf_op jit(solution)/shard_map/pallas_call | solution.py:296
Async XLA Ops:
  0.0 1.7 %collective-permute-start = (bf16[128,512]{1,0:T(8,128)(2,1)}, bf16[128,512]{1,0:T(8,128)(2,1)S(1)}, u32[]{:S(2)}, u32[]{:S(2)}) collective-permute-start(bf16[128,512]{1,0:T(8,128)(2,1)} %refs_0_.1), channel_id=1, source_target_pairs={{0,1},{1,0},{2,3},{3,2},{4,5},{5,4},{6,7},{7,6},{8,9},{9,8},{10,11... | collective-permute-start | bytes 393224 | tf_op jit(solution)/shard_map/ppermute | solution.py:255
  2.7 4.3 %collective-permute-start.1 = (f32[64,128]{1,0:T(8,128)S(1)}, f32[64,128]{1,0:T(8,128)S(1)}, u32[]{:S(2)}, u32[]{:S(2)}) collective-permute-start(f32[64,128]{1,0:T(8,128)S(1)} %shard_map.47.own_ref), channel_id=1, source_target_pairs={{0,3},{1,2},{2,1},{3,0},{4,7},{5,6},{6,5},{7,4},{8,11},{9,10},{10,... | collective-permute-start | bytes 98312 | tf_op jit(solution)/shard_map/ppermute | solution.py:287
  7.0 3.4 %collective-permute-start.2 = (f32[64,128]{1,0:T(8,128)S(1)}, f32[64,128]{1,0:T(8,128)S(1)}, u32[]{:S(2)}, u32[]{:S(2)}) collective-permute-start(f32[64,128]{1,0:T(8,128)S(1)} %shard_map.48.own_ref), channel_id=1, source_target_pairs={{0,5},{1,4},{2,7},{3,6},{4,1},{5,0},{6,3},{7,2},{8,13},{9,12},{10,... | collective-permute-start | bytes 98312 | tf_op jit(solution)/shard_map/ppermute | solution.py:287
  10.5 4.4 %collective-permute-start.3 = (f32[64,128]{1,0:T(8,128)S(1)}, f32[64,128]{1,0:T(8,128)S(1)}, u32[]{:S(2)}, u32[]{:S(2)}) collective-permute-start(f32[64,128]{1,0:T(8,128)S(1)} %shard_map.49.own_ref), channel_id=1, source_target_pairs={{0,9},{1,8},{2,11},{3,10},{4,13},{5,12},{6,15},{7,14},{8,1},{9,0},... | collective-permute-start | bytes 98312 | tf_op jit(solution)/shard_map/ppermute | solution.py:287
  15.0 1.2 %collective-permute-start.4 = (f32[32,128]{1,0:T(8,128)S(1)}, f32[32,128]{1,0:T(8,128)S(1)}, u32[]{:S(2)}, u32[]{:S(2)}) collective-permute-start(f32[32,128]{1,0:T(8,128)S(1)} %get-tuple-element.20), channel_id=1, source_target_pairs={{0,1},{1,0},{2,3},{3,2},{4,5},{5,4},{6,7},{7,6},{8,9},{9,8},{10,11... | collective-permute-start | bytes 49160 | tf_op jit(solution)/shard_map/ppermute | solution.py:301

commit v7 on v0

--- a/solution.py
+++ b/solution.py
@@ -26,10 +26,9 @@
     return -(-columns // LANES)
 
 
-def later(tiles, shift, count):
-    source = iota(shift.shape, 1) - shift
+def later(tiles, source, count):
     index = source & (LANES - 1)
-    zero = jnp.zeros(shift.shape, jnp.float32)
+    zero = jnp.zeros(source.shape, jnp.float32)
     spun = [zero] + [turned(tile, index, 1) for tile in tiles]
     return [jnp.where(source >= 0, spun[b + 1], spun[b]) for b in range(count)]
 
@@ -40,11 +39,9 @@
     while reach:
         first = row & reach == 0
         tiles = [
-            jnp.where(
-                first,
-                a + pltpu.roll(a, SUBLANES - reach, 0),
-                b + pltpu.roll(b, reach, 0),
-            )
+            jnp.where(first, a, b) + pltpu.roll(jnp.where(first, b, a), reach, 0)
+            if 2 * reach == SUBLANES
+            else jnp.where(first, a + pltpu.roll(a, SUBLANES - reach, 0), b + pltpu.roll(b, reach, 0))
             for a, b in zip(tiles[:reach], tiles[reach:])
         ]
         reach //= 2
@@ -110,14 +107,14 @@
     ]
     count = len(parts) // 2
     for i in range(count):
-        shifts_ref[i * rows : (i + 1) * rows, :] = spread[i].astype(jnp.int32)
+        shifts_ref[i * rows : (i + 1) * rows, :] = lane - spread[i].astype(jnp.int32)
     gain_ref[...] = (spread[count] + spread[count + 1] + spread[count + 2]) * (1.0 / WINDOW)
     kept = (SUBLANES, trials)
     kept = iota(kept, 1) == iota(kept, 0) * 2 + parity
     for l in range(cross_levels):
         step = jnp.sum(jnp.where(kept, cd_ref[l : l + 1, :].astype(jnp.float32), 0.0), axis=1, keepdims=True)
         step = jnp.broadcast_to(step, (SUBLANES, LANES)).astype(jnp.int32)
-        steps_ref[l * SUBLANES : (l + 1) * SUBLANES, :] = step
+        steps_ref[l * SUBLANES : (l + 1) * SUBLANES, :] = iota(step.shape, 1) - step
     copies[-1].wait()
 
 

time: 17.1 us -> 17.1 us (level)
  no operation moved by 1% of the time
where the time goes in v7:
time: 17.1 us; the launch traced here: 16.9 us
  starting transfers between devices  8.17 us (48%)
  waiting for transfers between devices  5.84 us (34%)
  Pallas kernels  2.82 us (16%)
    ppermute x3, starting transfers between devices, shards(): lax.ppermute(plane, ('sub', 'tm'), [(i, i ^ mask) for i in range(subs * s...  7.3 us
    ppermute x3, waiting for transfers between devices, shards(): lax.ppermute(plane, ('sub', 'tm'), [(i, i ^ mask) for i in range(subs * s...  4.8 us
    pallas_call x1, Pallas kernels, shards(): pl.pallas_call(table_kernel, out_shape=(jax.ShapeDtypeStruct(filterbank.s...  0.99 us
    pallas_call x1, Pallas kernels, shards(): pl.pallas_call(functools.partial(plane_kernel, trials), out_shape=tiled(s...  0.97 us
    ppermute x1, waiting for transfers between devices, shards(): lax.ppermute(send, 'tm', swap)  0.84 us
    pallas_call x1, Pallas kernels, shards(): call(functools.partial(last_kernel, cross_levels), out_shape=jax.ShapeDty...  0.63 us
    ppermute x1, starting transfers between devices, shards(): other = lax.ppermute(filterbank, 'tm', swap)  0.45 us
    ppermute x1, starting transfers between devices, shards(): lax.ppermute(send, 'tm', swap)  0.42 us
  transfers between devices with their start and end apart: 5, of which 5 were waited for; matrix products, arithmetic and copies ran while one was open for 0% of the time, Pallas kernels for 6%

profile of v7, /device:TPU:0, one launch (start us, length us, event | category | flops | bytes accessed | tf_op | source)
XLA Modules:
  0.0 16.9 jit_solution(17744742427866369941)
XLA Ops:
  0.0 0.5 %collective-permute-start = (bf16[128,512]{1,0:T(8,128)(2,1)}, bf16[128,512]{1,0:T(8,128)(2,1)S(1)}, u32[]{:S(2)}, u32[]{:S(2)}) collective-permute-start(bf16[128,512]{1,0:T(8,128)(2,1)} %refs_0_.1), channel_id=1, source_target_pairs={{0,1},{1,0},{2,3},{3,2},{4,5},{5,4},{6,7},{7,6},{8,9},{9,8},{10,11... | collective-permute-start | bytes 393224 | tf_op jit(solution)/shard_map/ppermute | solution.py:233
  0.5 1.0 %shard_map.46 = (bf16[128,512]{1,0:T(8,128)(2,1)S(1)}, s32[384,128]{1,0:T(8,128)S(1)}, f32[128,128]{1,0:T(8,128)S(1)}, s32[24,128]{1,0:T(8,128)S(1)}, bf16[512,256]{1,0:T(8,128)(2,1)S(1)}) custom-call(bf16[128,512]{1,0:T(8,128)(2,1)} %refs_0_.1, f32[1,128]{1,0:T(1,128)} %bitcast.1, s32[7,128]{1,0:T(8,128)} %refs_2_.1, s32[3,16]{1,0:T(4,128)} %refs_3_.1), custom_call_target="tpu_custom_call" | custom-call | tf_op jit(solution)/shard_map/pallas_call | solution.py:235
  1.4 0.2 %collective-permute-done.other_ref = bf16[128,512]{1,0:T(8,128)(2,1)S(1)} collective-permute-done((bf16[128,512]{1,0:T(8,128)(2,1)}, bf16[128,512]{1,0:T(8,128)(2,1)S(1)}, u32[]{:S(2)}, u32[]{:S(2)}) %collective-permute-start) | collective-permute-done | bytes 131104 | tf_op jit(solution)/shard_map/ppermute | solution.py:233
  1.7 1.0 %shard_map.47.own_ref = f32[64,128]{1,0:T(8,128)S(1)} custom-call(bf16[128,512]{1,0:T(8,128)(2,1)S(1)} %get-tuple-element.12.own_ref, bf16[128,512]{1,0:T(8,128)(2,1)S(1)} %collective-permute-done.other_ref, s32[384,128]{1,0:T(8,128)S(1)} %get-tuple-element.13.shifts_ref, f32[128,128]{1,0:T(8,128)S(1)} %get-tuple-element.14.gain_ref, ...), custom_call_target="tpu_custom_call" | custom-call | tf_op jit(solution)/shard_map/pallas_call | solution.py:250
  2.6 2.7 %collective-permute-start.1 = (f32[64,128]{1,0:T(8,128)S(1)}, f32[64,128]{1,0:T(8,128)S(1)}, u32[]{:S(2)}, u32[]{:S(2)}) collective-permute-start(f32[64,128]{1,0:T(8,128)S(1)} %shard_map.47.own_ref), channel_id=1, source_target_pairs={{0,3},{1,2},{2,1},{3,0},{4,7},{5,6},{6,5},{7,4},{8,11},{9,10},{10,... | collective-permute-start | bytes 98312 | tf_op jit(solution)/shard_map/ppermute | solution.py:264
  5.3 1.6 %collective-permute-done.1.there_ref = f32[64,128]{1,0:T(8,128)S(1)} collective-permute-done((f32[64,128]{1,0:T(8,128)S(1)}, f32[64,128]{1,0:T(8,128)S(1)}, u32[]{:S(2)}, u32[]{:S(2)}) %collective-permute-start.1) | collective-permute-done | bytes 32800 | tf_op jit(solution)/shard_map/ppermute | solution.py:264
  6.9 0.1 shard_map.48.own_ref
  7.0 1.9 %collective-permute-start.2 = (f32[64,128]{1,0:T(8,128)S(1)}, f32[64,128]{1,0:T(8,128)S(1)}, u32[]{:S(2)}, u32[]{:S(2)}) collective-permute-start(f32[64,128]{1,0:T(8,128)S(1)} %shard_map.48.own_ref), channel_id=1, source_target_pairs={{0,5},{1,4},{2,7},{3,6},{4,1},{5,0},{6,3},{7,2},{8,13},{9,12},{10,... | collective-permute-start | bytes 98312 | tf_op jit(solution)/shard_map/ppermute | solution.py:264
  8.8 1.6 %collective-permute-done.2.there_ref = f32[64,128]{1,0:T(8,128)S(1)} collective-permute-done((f32[64,128]{1,0:T(8,128)S(1)}, f32[64,128]{1,0:T(8,128)S(1)}, u32[]{:S(2)}, u32[]{:S(2)}) %collective-permute-start.2) | collective-permute-done | bytes 32800 | tf_op jit(solution)/shard_map/ppermute | solution.py:264
  10.4 0.1 shard_map.49.own_ref
  10.5 2.8 %collective-permute-start.3 = (f32[64,128]{1,0:T(8,128)S(1)}, f32[64,128]{1,0:T(8,128)S(1)}, u32[]{:S(2)}, u32[]{:S(2)}) collective-permute-start(f32[64,128]{1,0:T(8,128)S(1)} %shard_map.49.own_ref), channel_id=1, source_target_pairs={{0,9},{1,8},{2,11},{3,10},{4,13},{5,12},{6,15},{7,14},{8,1},{9,0},... | collective-permute-start | bytes 98312 | tf_op jit(solution)/shard_map/ppermute | solution.py:264
  13.3 1.6 %collective-permute-done.3.there_ref = f32[64,128]{1,0:T(8,128)S(1)} collective-permute-done((f32[64,128]{1,0:T(8,128)S(1)}, f32[64,128]{1,0:T(8,128)S(1)}, u32[]{:S(2)}, u32[]{:S(2)}) %collective-permute-start.3) | collective-permute-done | bytes 32800 | tf_op jit(solution)/shard_map/ppermute | solution.py:264
  14.9 0.1 shard_map.50
  15.0 0.4 %collective-permute-start.4 = (f32[32,128]{1,0:T(8,128)S(1)}, f32[32,128]{1,0:T(8,128)S(1)}, u32[]{:S(2)}, u32[]{:S(2)}) collective-permute-start(f32[32,128]{1,0:T(8,128)S(1)} %get-tuple-element.18), channel_id=1, source_target_pairs={{0,1},{1,0},{2,3},{3,2},{4,5},{5,4},{6,7},{7,6},{8,9},{9,8},{10,11... | collective-permute-start | bytes 49160 | tf_op jit(solution)/shard_map/ppermute | solution.py:278
  15.4 0.8 %collective-permute-done.4.there_ref = f32[32,128]{1,0:T(8,128)S(1)} collective-permute-done((f32[32,128]{1,0:T(8,128)S(1)}, f32[32,128]{1,0:T(8,128)S(1)}, u32[]{:S(2)}, u32[]{:S(2)}) %collective-permute-start.4) | collective-permute-done | bytes 16416 | tf_op jit(solution)/shard_map/ppermute | solution.py:278
  16.2 0.6 %shard_map.51 = f32[16,512]{1,0:T(8,128)} custom-call(f32[32,128]{1,0:T(8,128)S(1)} %get-tuple-element.17.keep_ref, f32[32,128]{1,0:T(8,128)S(1)} %collective-permute-done.4.there_ref), custom_call_target="tpu_custom_call" | custom-call | tf_op jit(solution)/shard_map/pallas_call | solution.py:273
Async XLA Ops:
  0.0 1.6 %collective-permute-start = (bf16[128,512]{1,0:T(8,128)(2,1)}, bf16[128,512]{1,0:T(8,128)(2,1)S(1)}, u32[]{:S(2)}, u32[]{:S(2)}) collective-permute-start(bf16[128,512]{1,0:T(8,128)(2,1)} %refs_0_.1), channel_id=1, source_target_pairs={{0,1},{1,0},{2,3},{3,2},{4,5},{5,4},{6,7},{7,6},{8,9},{9,8},{10,11... | collective-permute-start | bytes 393224 | tf_op jit(solution)/shard_map/ppermute | solution.py:233
  2.6 4.3 %collective-permute-start.1 = (f32[64,128]{1,0:T(8,128)S(1)}, f32[64,128]{1,0:T(8,128)S(1)}, u32[]{:S(2)}, u32[]{:S(2)}) collective-permute-start(f32[64,128]{1,0:T(8,128)S(1)} %shard_map.47.own_ref), channel_id=1, source_target_pairs={{0,3},{1,2},{2,1},{3,0},{4,7},{5,6},{6,5},{7,4},{8,11},{9,10},{10,... | collective-permute-start | bytes 98312 | tf_op jit(solution)/shard_map/ppermute | solution.py:264
  7.0 3.5 %collective-permute-start.2 = (f32[64,128]{1,0:T(8,128)S(1)}, f32[64,128]{1,0:T(8,128)S(1)}, u32[]{:S(2)}, u32[]{:S(2)}) collective-permute-start(f32[64,128]{1,0:T(8,128)S(1)} %shard_map.48.own_ref), channel_id=1, source_target_pairs={{0,5},{1,4},{2,7},{3,6},{4,1},{5,0},{6,3},{7,2},{8,13},{9,12},{10,... | collective-permute-start | bytes 98312 | tf_op jit(solution)/shard_map/ppermute | solution.py:264
  10.5 4.4 %collective-permute-start.3 = (f32[64,128]{1,0:T(8,128)S(1)}, f32[64,128]{1,0:T(8,128)S(1)}, u32[]{:S(2)}, u32[]{:S(2)}) collective-permute-start(f32[64,128]{1,0:T(8,128)S(1)} %shard_map.49.own_ref), channel_id=1, source_target_pairs={{0,9},{1,8},{2,11},{3,10},{4,13},{5,12},{6,15},{7,14},{8,1},{9,0},... | collective-permute-start | bytes 98312 | tf_op jit(solution)/shard_map/ppermute | solution.py:264
  15.0 1.3 %collective-permute-start.4 = (f32[32,128]{1,0:T(8,128)S(1)}, f32[32,128]{1,0:T(8,128)S(1)}, u32[]{:S(2)}, u32[]{:S(2)}) collective-permute-start(f32[32,128]{1,0:T(8,128)S(1)} %get-tuple-element.18), channel_id=1, source_target_pairs={{0,1},{1,0},{2,3},{3,2},{4,5},{5,4},{6,7},{7,6},{8,9},{9,8},{10,11... | collective-permute-start | bytes 49160 | tf_op jit(solution)/shard_map/ppermute | solution.py:278

commit v8 on v0

--- a/solution.py
+++ b/solution.py
@@ -147,21 +147,18 @@
         level_ref[block * rows : (block + 1) * rows, :] = got[:, :LANES]
         level_ref[(block + 1) * rows : (block + 2) * rows, :] = got[:, LANES:]
 
-    bands = []
-    for e in range(trials):
+    def band(e):
         scale = gain_ref[e * SUBLANES : (e + 1) * SUBLANES, :]
-        bands.append(
-            [level_ref[pl.ds(block * rows + e, SUBLANES, stride=trials), :] * scale for block in range(blocks)]
-        )
-    plane = [bands]
+        return [level_ref[pl.ds(block * rows + e, SUBLANES, stride=trials), :] * scale for block in range(blocks)]
 
     def merged(low, high, at_row):
         moved = later(high, shifts_ref[at_row : at_row + SUBLANES, :], blocks)
         return [a + b for a, b in zip(low, moved)]
 
-    for m in range(grow):
+    plane = [[merged(band(2 * e), band(2 * e + 1), e * SUBLANES) for e in range(trials // 2)]]
+    for m in range(1, grow):
         old, plane = plane, []
-        for c in range(2 if m else 1):
+        for c in range(2):
             for i, held in enumerate(old):
                 j = c * len(old) + i
                 starts = [m * rows // 2 + ((e << m) + j) * SUBLANES for e in range(len(held) // 2)]

time: 17.1 us -> 17.1 us (level)
  no operation moved by 1% of the time
where the time goes in v8:
time: 17.1 us; the launch traced here: 16.9 us
  starting transfers between devices  8.17 us (48%)
  waiting for transfers between devices  5.84 us (34%)
  Pallas kernels  2.83 us (17%)
    ppermute x3, starting transfers between devices, shards(): lax.ppermute(plane, ('sub', 'tm'), [(i, i ^ mask) for i in range(subs * s...  7.3 us
    ppermute x3, waiting for transfers between devices, shards(): lax.ppermute(plane, ('sub', 'tm'), [(i, i ^ mask) for i in range(subs * s...  4.8 us
    pallas_call x1, Pallas kernels, shards(): pl.pallas_call(table_kernel, out_shape=(jax.ShapeDtypeStruct(filterbank.s...  0.99 us
    pallas_call x1, Pallas kernels, shards(): pl.pallas_call(functools.partial(plane_kernel, trials), out_shape=tiled(s...  0.97 us
    ppermute x1, waiting for transfers between devices, shards(): lax.ppermute(send, 'tm', swap)  0.84 us
    pallas_call x1, Pallas kernels, shards(): call(functools.partial(last_kernel, cross_levels), out_shape=jax.ShapeDty...  0.63 us
    ppermute x1, starting transfers between devices, shards(): other = lax.ppermute(filterbank, 'tm', swap)  0.45 us
    ppermute x1, starting transfers between devices, shards(): lax.ppermute(send, 'tm', swap)  0.42 us
  transfers between devices with their start and end apart: 5, of which 5 were waited for; matrix products, arithmetic and copies ran while one was open for 0% of the time, Pallas kernels for 6%

profile of v8, /device:TPU:0, one launch (start us, length us, event | category | flops | bytes accessed | tf_op | source)
XLA Modules:
  0.0 16.9 jit_solution(8258872430106052774)
XLA Ops:
  0.0 0.5 %collective-permute-start = (bf16[128,512]{1,0:T(8,128)(2,1)}, bf16[128,512]{1,0:T(8,128)(2,1)S(1)}, u32[]{:S(2)}, u32[]{:S(2)}) collective-permute-start(bf16[128,512]{1,0:T(8,128)(2,1)} %refs_0_.1), channel_id=1, source_target_pairs={{0,1},{1,0},{2,3},{3,2},{4,5},{5,4},{6,7},{7,6},{8,9},{9,8},{10,11... | collective-permute-start | bytes 393224 | tf_op jit(solution)/shard_map/ppermute | solution.py:233
  0.5 1.0 %shard_map.46 = (bf16[128,512]{1,0:T(8,128)(2,1)S(1)}, s32[384,128]{1,0:T(8,128)S(1)}, f32[128,128]{1,0:T(8,128)S(1)}, s32[24,128]{1,0:T(8,128)S(1)}, bf16[512,256]{1,0:T(8,128)(2,1)S(1)}) custom-call(bf16[128,512]{1,0:T(8,128)(2,1)} %refs_0_.1, f32[1,128]{1,0:T(1,128)} %bitcast.1, s32[7,128]{1,0:T(8,128)} %refs_2_.1, s32[3,16]{1,0:T(4,128)} %refs_3_.1), custom_call_target="tpu_custom_call" | custom-call | tf_op jit(solution)/shard_map/pallas_call | solution.py:235
  1.4 0.2 %collective-permute-done.other_ref = bf16[128,512]{1,0:T(8,128)(2,1)S(1)} collective-permute-done((bf16[128,512]{1,0:T(8,128)(2,1)}, bf16[128,512]{1,0:T(8,128)(2,1)S(1)}, u32[]{:S(2)}, u32[]{:S(2)}) %collective-permute-start) | collective-permute-done | bytes 131104 | tf_op jit(solution)/shard_map/ppermute | solution.py:233
  1.7 1.0 %shard_map.47.own_ref = f32[64,128]{1,0:T(8,128)S(1)} custom-call(bf16[128,512]{1,0:T(8,128)(2,1)S(1)} %get-tuple-element.12.own_ref, bf16[128,512]{1,0:T(8,128)(2,1)S(1)} %collective-permute-done.other_ref, s32[384,128]{1,0:T(8,128)S(1)} %get-tuple-element.13.shifts_ref, f32[128,128]{1,0:T(8,128)S(1)} %get-tuple-element.14.gain_ref, ...), custom_call_target="tpu_custom_call" | custom-call | tf_op jit(solution)/shard_map/pallas_call | solution.py:250
  2.6 2.7 %collective-permute-start.1 = (f32[64,128]{1,0:T(8,128)S(1)}, f32[64,128]{1,0:T(8,128)S(1)}, u32[]{:S(2)}, u32[]{:S(2)}) collective-permute-start(f32[64,128]{1,0:T(8,128)S(1)} %shard_map.47.own_ref), channel_id=1, source_target_pairs={{0,3},{1,2},{2,1},{3,0},{4,7},{5,6},{6,5},{7,4},{8,11},{9,10},{10,... | collective-permute-start | bytes 98312 | tf_op jit(solution)/shard_map/ppermute | solution.py:264
  5.3 1.6 %collective-permute-done.1.there_ref = f32[64,128]{1,0:T(8,128)S(1)} collective-permute-done((f32[64,128]{1,0:T(8,128)S(1)}, f32[64,128]{1,0:T(8,128)S(1)}, u32[]{:S(2)}, u32[]{:S(2)}) %collective-permute-start.1) | collective-permute-done | bytes 32800 | tf_op jit(solution)/shard_map/ppermute | solution.py:264
  6.9 0.1 shard_map.48.own_ref
  7.0 1.9 %collective-permute-start.2 = (f32[64,128]{1,0:T(8,128)S(1)}, f32[64,128]{1,0:T(8,128)S(1)}, u32[]{:S(2)}, u32[]{:S(2)}) collective-permute-start(f32[64,128]{1,0:T(8,128)S(1)} %shard_map.48.own_ref), channel_id=1, source_target_pairs={{0,5},{1,4},{2,7},{3,6},{4,1},{5,0},{6,3},{7,2},{8,13},{9,12},{10,... | collective-permute-start | bytes 98312 | tf_op jit(solution)/shard_map/ppermute | solution.py:264
  8.8 1.6 %collective-permute-done.2.there_ref = f32[64,128]{1,0:T(8,128)S(1)} collective-permute-done((f32[64,128]{1,0:T(8,128)S(1)}, f32[64,128]{1,0:T(8,128)S(1)}, u32[]{:S(2)}, u32[]{:S(2)}) %collective-permute-start.2) | collective-permute-done | bytes 32800 | tf_op jit(solution)/shard_map/ppermute | solution.py:264
  10.4 0.1 shard_map.49.own_ref
  10.5 2.8 %collective-permute-start.3 = (f32[64,128]{1,0:T(8,128)S(1)}, f32[64,128]{1,0:T(8,128)S(1)}, u32[]{:S(2)}, u32[]{:S(2)}) collective-permute-start(f32[64,128]{1,0:T(8,128)S(1)} %shard_map.49.own_ref), channel_id=1, source_target_pairs={{0,9},{1,8},{2,11},{3,10},{4,13},{5,12},{6,15},{7,14},{8,1},{9,0},... | collective-permute-start | bytes 98312 | tf_op jit(solution)/shard_map/ppermute | solution.py:264
  13.3 1.6 %collective-permute-done.3.there_ref = f32[64,128]{1,0:T(8,128)S(1)} collective-permute-done((f32[64,128]{1,0:T(8,128)S(1)}, f32[64,128]{1,0:T(8,128)S(1)}, u32[]{:S(2)}, u32[]{:S(2)}) %collective-permute-start.3) | collective-permute-done | bytes 32800 | tf_op jit(solution)/shard_map/ppermute | solution.py:264
  14.9 0.1 shard_map.50
  15.0 0.4 %collective-permute-start.4 = (f32[32,128]{1,0:T(8,128)S(1)}, f32[32,128]{1,0:T(8,128)S(1)}, u32[]{:S(2)}, u32[]{:S(2)}) collective-permute-start(f32[32,128]{1,0:T(8,128)S(1)} %get-tuple-element.18), channel_id=1, source_target_pairs={{0,1},{1,0},{2,3},{3,2},{4,5},{5,4},{6,7},{7,6},{8,9},{9,8},{10,11... | collective-permute-start | bytes 49160 | tf_op jit(solution)/shard_map/ppermute | solution.py:278
  15.4 0.8 %collective-permute-done.4.there_ref = f32[32,128]{1,0:T(8,128)S(1)} collective-permute-done((f32[32,128]{1,0:T(8,128)S(1)}, f32[32,128]{1,0:T(8,128)S(1)}, u32[]{:S(2)}, u32[]{:S(2)}) %collective-permute-start.4) | collective-permute-done | bytes 16416 | tf_op jit(solution)/shard_map/ppermute | solution.py:278
  16.2 0.6 %shard_map.51 = f32[16,512]{1,0:T(8,128)} custom-call(f32[32,128]{1,0:T(8,128)S(1)} %get-tuple-element.17.keep_ref, f32[32,128]{1,0:T(8,128)S(1)} %collective-permute-done.4.there_ref), custom_call_target="tpu_custom_call" | custom-call | tf_op jit(solution)/shard_map/pallas_call | solution.py:273
Async XLA Ops:
  0.0 1.6 %collective-permute-start = (bf16[128,512]{1,0:T(8,128)(2,1)}, bf16[128,512]{1,0:T(8,128)(2,1)S(1)}, u32[]{:S(2)}, u32[]{:S(2)}) collective-permute-start(bf16[128,512]{1,0:T(8,128)(2,1)} %refs_0_.1), channel_id=1, source_target_pairs={{0,1},{1,0},{2,3},{3,2},{4,5},{5,4},{6,7},{7,6},{8,9},{9,8},{10,11... | collective-permute-start | bytes 393224 | tf_op jit(solution)/shard_map/ppermute | solution.py:233
  2.6 4.3 %collective-permute-start.1 = (f32[64,128]{1,0:T(8,128)S(1)}, f32[64,128]{1,0:T(8,128)S(1)}, u32[]{:S(2)}, u32[]{:S(2)}) collective-permute-start(f32[64,128]{1,0:T(8,128)S(1)} %shard_map.47.own_ref), channel_id=1, source_target_pairs={{0,3},{1,2},{2,1},{3,0},{4,7},{5,6},{6,5},{7,4},{8,11},{9,10},{10,... | collective-permute-start | bytes 98312 | tf_op jit(solution)/shard_map/ppermute | solution.py:264
  7.0 3.5 %collective-permute-start.2 = (f32[64,128]{1,0:T(8,128)S(1)}, f32[64,128]{1,0:T(8,128)S(1)}, u32[]{:S(2)}, u32[]{:S(2)}) collective-permute-start(f32[64,128]{1,0:T(8,128)S(1)} %shard_map.48.own_ref), channel_id=1, source_target_pairs={{0,5},{1,4},{2,7},{3,6},{4,1},{5,0},{6,3},{7,2},{8,13},{9,12},{10,... | collective-permute-start | bytes 98312 | tf_op jit(solution)/shard_map/ppermute | solution.py:264
  10.5 4.4 %collective-permute-start.3 = (f32[64,128]{1,0:T(8,128)S(1)}, f32[64,128]{1,0:T(8,128)S(1)}, u32[]{:S(2)}, u32[]{:S(2)}) collective-permute-start(f32[64,128]{1,0:T(8,128)S(1)} %shard_map.49.own_ref), channel_id=1, source_target_pairs={{0,9},{1,8},{2,11},{3,10},{4,13},{5,12},{6,15},{7,14},{8,1},{9,0},... | collective-permute-start | bytes 98312 | tf_op jit(solution)/shard_map/ppermute | solution.py:264
  15.0 1.3 %collective-permute-start.4 = (f32[32,128]{1,0:T(8,128)S(1)}, f32[32,128]{1,0:T(8,128)S(1)}, u32[]{:S(2)}, u32[]{:S(2)}) collective-permute-start(f32[32,128]{1,0:T(8,128)S(1)} %get-tuple-element.18), channel_id=1, source_target_pairs={{0,1},{1,0},{2,3},{3,2},{4,5},{5,4},{6,7},{7,6},{8,9},{9,8},{10,11... | collective-permute-start | bytes 49160 | tf_op jit(solution)/shard_map/ppermute | solution.py:278

commit v9 on v8

--- a/solution.py
+++ b/solution.py
@@ -171,7 +171,7 @@
 
 def row_half(cross_levels):
     half = lax.axis_index("tm")
-    for level in range(cross_levels):
+    for level in range(cross_levels - 1):
         half = half ^ (lax.axis_index("sub") >> level & 1)
     return half
 
@@ -260,7 +260,7 @@
     )(own, other, shifts, gain, band)
     for level in range(cross_levels):
         last = level == cross_levels - 1
-        mask = spans << level | 1
+        mask = spans << level | (0 if last else 1)
         there = lax.ppermute(plane, ("sub", "tm"), [(i, i ^ mask) for i in range(subs * spans)])
         scale = 1.0 / math.sqrt(rows * subs) if last else None
         plane = call(

time: 17.1 us -> 17.5 us (1.023)
  waiting for transfers between devices: 5.84 us -> 6.47 us
    ppermute x1, starting transfers between devices: 0.42 us -> 0.07 us  [shards(): lax.ppermute(send, 'tm', swap)]
    ppermute x1, waiting for transfers between devices: 0.84 us -> 1.17 us  [shards(): lax.ppermute(send, 'tm', swap)]
    ppermute x3, waiting for transfers between devices: 4.8 us -> 5.09 us  [shards(): lax.ppermute(plane, ('sub', 'tm'), [(i, i ^ mask) for i in range(subs * s...]
    ppermute x3, starting transfers between devices: 7.3 us -> 7.54 us  [shards(): lax.ppermute(plane, ('sub', 'tm'), [(i, i ^ mask) for i in range(subs * s...]
where the time goes in v9:
time: 17.5 us; the launch traced here: 17.4 us
  starting transfers between devices  8.06 us (46%)
  waiting for transfers between devices  6.47 us (37%)
  Pallas kernels  2.83 us (16%)
    ppermute x3, starting transfers between devices, shards(): lax.ppermute(plane, ('sub', 'tm'), [(i, i ^ mask) for i in range(subs * s...  7.54 us
    ppermute x3, waiting for transfers between devices, shards(): lax.ppermute(plane, ('sub', 'tm'), [(i, i ^ mask) for i in range(subs * s...  5.09 us
    ppermute x1, waiting for transfers between devices, shards(): lax.ppermute(send, 'tm', swap)  1.17 us
    pallas_call x1, Pallas kernels, shards(): pl.pallas_call(table_kernel, out_shape=(jax.ShapeDtypeStruct(filterbank.s...  0.99 us
    pallas_call x1, Pallas kernels, shards(): pl.pallas_call(functools.partial(plane_kernel, trials), out_shape=tiled(s...  0.97 us
    pallas_call x1, Pallas kernels, shards(): call(functools.partial(last_kernel, cross_levels), out_shape=jax.ShapeDty...  0.63 us
    ppermute x1, starting transfers between devices, shards(): other = lax.ppermute(filterbank, 'tm', swap)  0.45 us
  transfers between devices with their start and end apart: 5, of which 5 were waited for; matrix products, arithmetic and copies ran while one was open for 0% of the time, Pallas kernels for 6%

profile of v9, /device:TPU:0, one launch (start us, length us, event | category | flops | bytes accessed | tf_op | source)
XLA Modules:
  0.0 17.4 jit_solution(11226707721430150007)
XLA Ops:
  0.0 0.5 %collective-permute-start = (bf16[128,512]{1,0:T(8,128)(2,1)}, bf16[128,512]{1,0:T(8,128)(2,1)S(1)}, u32[]{:S(2)}, u32[]{:S(2)}) collective-permute-start(bf16[128,512]{1,0:T(8,128)(2,1)} %refs_0_.1), channel_id=1, source_target_pairs={{0,1},{1,0},{2,3},{3,2},{4,5},{5,4},{6,7},{7,6},{8,9},{9,8},{10,11... | collective-permute-start | bytes 393224 | tf_op jit(solution)/shard_map/ppermute | solution.py:233
  0.5 1.0 %shard_map.46 = (bf16[128,512]{1,0:T(8,128)(2,1)S(1)}, s32[384,128]{1,0:T(8,128)S(1)}, f32[128,128]{1,0:T(8,128)S(1)}, s32[24,128]{1,0:T(8,128)S(1)}, bf16[512,256]{1,0:T(8,128)(2,1)S(1)}) custom-call(bf16[128,512]{1,0:T(8,128)(2,1)} %refs_0_.1, f32[1,128]{1,0:T(1,128)} %bitcast.1, s32[7,128]{1,0:T(8,128)} %refs_2_.1, s32[3,16]{1,0:T(4,128)} %refs_3_.1), custom_call_target="tpu_custom_call" | custom-call | tf_op jit(solution)/shard_map/pallas_call | solution.py:235
  1.4 0.2 %collective-permute-done.other_ref = bf16[128,512]{1,0:T(8,128)(2,1)S(1)} collective-permute-done((bf16[128,512]{1,0:T(8,128)(2,1)}, bf16[128,512]{1,0:T(8,128)(2,1)S(1)}, u32[]{:S(2)}, u32[]{:S(2)}) %collective-permute-start) | collective-permute-done | bytes 131104 | tf_op jit(solution)/shard_map/ppermute | solution.py:233
  1.7 1.0 %shard_map.47.own_ref = f32[64,128]{1,0:T(8,128)S(1)} custom-call(bf16[128,512]{1,0:T(8,128)(2,1)S(1)} %get-tuple-element.12.own_ref, bf16[128,512]{1,0:T(8,128)(2,1)S(1)} %collective-permute-done.other_ref, s32[384,128]{1,0:T(8,128)S(1)} %get-tuple-element.13.shifts_ref, f32[128,128]{1,0:T(8,128)S(1)} %get-tuple-element.14.gain_ref, ...), custom_call_target="tpu_custom_call" | custom-call | tf_op jit(solution)/shard_map/pallas_call | solution.py:250
  2.6 2.7 %collective-permute-start.1 = (f32[64,128]{1,0:T(8,128)S(1)}, f32[64,128]{1,0:T(8,128)S(1)}, u32[]{:S(2)}, u32[]{:S(2)}) collective-permute-start(f32[64,128]{1,0:T(8,128)S(1)} %shard_map.47.own_ref), channel_id=1, source_target_pairs={{0,3},{1,2},{2,1},{3,0},{4,7},{5,6},{6,5},{7,4},{8,11},{9,10},{10,... | collective-permute-start | bytes 98312 | tf_op jit(solution)/shard_map/ppermute | solution.py:264
  5.3 1.6 %collective-permute-done.1.there_ref = f32[64,128]{1,0:T(8,128)S(1)} collective-permute-done((f32[64,128]{1,0:T(8,128)S(1)}, f32[64,128]{1,0:T(8,128)S(1)}, u32[]{:S(2)}, u32[]{:S(2)}) %collective-permute-start.1) | collective-permute-done | bytes 32800 | tf_op jit(solution)/shard_map/ppermute | solution.py:264
  6.9 0.1 shard_map.48.own_ref
  7.0 1.9 %collective-permute-start.2 = (f32[64,128]{1,0:T(8,128)S(1)}, f32[64,128]{1,0:T(8,128)S(1)}, u32[]{:S(2)}, u32[]{:S(2)}) collective-permute-start(f32[64,128]{1,0:T(8,128)S(1)} %shard_map.48.own_ref), channel_id=1, source_target_pairs={{0,5},{1,4},{2,7},{3,6},{4,1},{5,0},{6,3},{7,2},{8,13},{9,12},{10,... | collective-permute-start | bytes 98312 | tf_op jit(solution)/shard_map/ppermute | solution.py:264
  8.8 1.6 %collective-permute-done.2.there_ref = f32[64,128]{1,0:T(8,128)S(1)} collective-permute-done((f32[64,128]{1,0:T(8,128)S(1)}, f32[64,128]{1,0:T(8,128)S(1)}, u32[]{:S(2)}, u32[]{:S(2)}) %collective-permute-start.2) | collective-permute-done | bytes 32800 | tf_op jit(solution)/shard_map/ppermute | solution.py:264
  10.4 0.1 shard_map.49.own_ref
  10.5 3.0 %collective-permute-start.3 = (f32[64,128]{1,0:T(8,128)S(1)}, f32[64,128]{1,0:T(8,128)S(1)}, u32[]{:S(2)}, u32[]{:S(2)}) collective-permute-start(f32[64,128]{1,0:T(8,128)S(1)} %shard_map.49.own_ref), channel_id=1, source_target_pairs={{0,8},{1,9},{2,10},{3,11},{4,12},{5,13},{6,14},{7,15},{8,0},{9,1},... | collective-permute-start | bytes 98312 | tf_op jit(solution)/shard_map/ppermute | solution.py:264
  13.5 1.9 %collective-permute-done.3.there_ref = f32[64,128]{1,0:T(8,128)S(1)} collective-permute-done((f32[64,128]{1,0:T(8,128)S(1)}, f32[64,128]{1,0:T(8,128)S(1)}, u32[]{:S(2)}, u32[]{:S(2)}) %collective-permute-start.3) | collective-permute-done | bytes 32800 | tf_op jit(solution)/shard_map/ppermute | solution.py:264
  15.4 0.1 shard_map.50
  15.5 0.1 collective-permute-start.4
  15.6 1.2 %collective-permute-done.4.there_ref = f32[32,128]{1,0:T(8,128)S(1)} collective-permute-done((f32[32,128]{1,0:T(8,128)S(1)}, f32[32,128]{1,0:T(8,128)S(1)}, u32[]{:S(2)}, u32[]{:S(2)}) %collective-permute-start.4) | collective-permute-done | bytes 16416 | tf_op jit(solution)/shard_map/ppermute | solution.py:278
  16.8 0.6 %shard_map.51 = f32[16,512]{1,0:T(8,128)} custom-call(f32[32,128]{1,0:T(8,128)S(1)} %get-tuple-element.17.keep_ref, f32[32,128]{1,0:T(8,128)S(1)} %collective-permute-done.4.there_ref), custom_call_target="tpu_custom_call" | custom-call | tf_op jit(solution)/shard_map/pallas_call | solution.py:273
Async XLA Ops:
  0.0 1.6 %collective-permute-start = (bf16[128,512]{1,0:T(8,128)(2,1)}, bf16[128,512]{1,0:T(8,128)(2,1)S(1)}, u32[]{:S(2)}, u32[]{:S(2)}) collective-permute-start(bf16[128,512]{1,0:T(8,128)(2,1)} %refs_0_.1), channel_id=1, source_target_pairs={{0,1},{1,0},{2,3},{3,2},{4,5},{5,4},{6,7},{7,6},{8,9},{9,8},{10,11... | collective-permute-start | bytes 393224 | tf_op jit(solution)/shard_map/ppermute | solution.py:233
  2.6 4.3 %collective-permute-start.1 = (f32[64,128]{1,0:T(8,128)S(1)}, f32[64,128]{1,0:T(8,128)S(1)}, u32[]{:S(2)}, u32[]{:S(2)}) collective-permute-start(f32[64,128]{1,0:T(8,128)S(1)} %shard_map.47.own_ref), channel_id=1, source_target_pairs={{0,3},{1,2},{2,1},{3,0},{4,7},{5,6},{6,5},{7,4},{8,11},{9,10},{10,... | collective-permute-start | bytes 98312 | tf_op jit(solution)/shard_map/ppermute | solution.py:264
  7.0 3.5 %collective-permute-start.2 = (f32[64,128]{1,0:T(8,128)S(1)}, f32[64,128]{1,0:T(8,128)S(1)}, u32[]{:S(2)}, u32[]{:S(2)}) collective-permute-start(f32[64,128]{1,0:T(8,128)S(1)} %shard_map.48.own_ref), channel_id=1, source_target_pairs={{0,5},{1,4},{2,7},{3,6},{4,1},{5,0},{6,3},{7,2},{8,13},{9,12},{10,... | collective-permute-start | bytes 98312 | tf_op jit(solution)/shard_map/ppermute | solution.py:264
  10.5 4.9 %collective-permute-start.3 = (f32[64,128]{1,0:T(8,128)S(1)}, f32[64,128]{1,0:T(8,128)S(1)}, u32[]{:S(2)}, u32[]{:S(2)}) collective-permute-start(f32[64,128]{1,0:T(8,128)S(1)} %shard_map.49.own_ref), channel_id=1, source_target_pairs={{0,8},{1,9},{2,10},{3,11},{4,12},{5,13},{6,14},{7,15},{8,0},{9,1},... | collective-permute-start | bytes 98312 | tf_op jit(solution)/shard_map/ppermute | solution.py:264
  15.5 1.2 %collective-permute-start.4 = (f32[32,128]{1,0:T(8,128)S(1)}, f32[32,128]{1,0:T(8,128)S(1)}, u32[]{:S(2)}, u32[]{:S(2)}) collective-permute-start(f32[32,128]{1,0:T(8,128)S(1)} %get-tuple-element.18), channel_id=1, source_target_pairs={{0,1},{1,0},{2,3},{3,2},{4,5},{5,4},{6,7},{7,6},{8,9},{9,8},{10,11... | collective-permute-start | bytes 49160 | tf_op jit(solution)/shard_map/ppermute | solution.py:278
